TPU v7x, 512 devices: a whole 4x8x8 slice. The times are simulated.
512 devices in a mesh: seq: 64 (over z, x, core), head: 8 (over y).
Axes of the slice: x: 4, y: 8, z: 8, core: 2. Of those that a mesh axis runs over, the one named last changes fastest.
Arguments:
- loaded: bfloat16 [8192, 2048], P('seq', 'head'), may hold values from -6 to 6
- out_grad: bfloat16 [8192, 2048], P('seq', 'head'), may hold values from -6 to 6
- w_query: bfloat16 [2048, 2048], P(None, 'head'), may hold values from -0.125 to 0.125
- w_key: bfloat16 [2048, 2048], P(None, 'head'), may hold values from -0.125 to 0.125
- w_value: bfloat16 [2048, 2048], P(None, 'head'), may hold values from -0.125 to 0.125
- w_beta: bfloat16 [2048, 16], P(None, 'head'), may hold values from -0.125 to 0.125
- beta_max: float32 [16], P('head'), may hold values from 0.015625 to 1
- out_gain: float32 [128], replicated, may hold values from 0.1 to 1.9
- clip_lengths: int32 [16], replicated, may hold values from 1 to 2048, 8192 in all
- delay_offsets: int32 [4], replicated, may hold values from 0 to 3, each once
- block_order: int32 [64, 64], P('seq'), may hold values from 0 to 63, each once within a row
Outputs:
- head_out: bfloat16 [8192, 2048], P('seq', 'head')
- input_grad: bfloat16 [8192, 2048], P('seq', 'head')
Inputs may be any that keep to these rules, and one draw needn't show every extreme that they name: `clip_lengths`: the clip lengths sum to 8192; the longest is exactly 2048. `delay_offsets`: each codebook has a different delay. `block_order`: each row is a permutation of 0 to 63.
All inputs are finite; a program needn't handle non-finite values.
Results may differ from a plain program's by a relative error of at most 0.022.
Values may be sent and summed in bfloat16 or wider, within the bound.
A program may use at most 128 MiB of HBM per device.

v0:
```python
import jax
import jax.numpy as jnp
from jax import lax
from jax.sharding import PartitionSpec as P

SPAN = 128


EPSILON = 1e-06
HIGHEST = lax.Precision.HIGHEST


def from_behind(x, axis, by):
    count = lax.axis_size(axis)
    pairs = [(i, i + by) for i in range(count) if 0 <= i + by < count]
    return lax.ppermute(x, axis, pairs)


def prefix(x, axis, join, neutral):
    place = lax.axis_index(axis)
    gathered = jax.tree.map(
        lambda a, kind: lax.all_gather(a.astype(kind), axis), x, (jnp.bfloat16, jnp.bfloat16)
    )
    state = jax.tree.map(lambda a, e: jnp.zeros_like(a) + jnp.asarray(e, a.dtype), x, neutral)

    def one(turn, state):
        return join(
            state,
            jax.tree.map(
                lambda a, own: lax.dynamic_index_in_dim(a, turn, 0, False).astype(own.dtype),
                gathered,
                x,
            ),
        )

    return lax.fori_loop(0, place, one, state)


def prefix_2(x, axis, combine, identity):
    count, here = (lax.axis_size(axis), lax.axis_index(axis))
    everything = jax.tree.map(
        lambda part, kind: lax.all_gather(part.astype(kind), axis),
        x,
        jax.tree.map(lambda a: jnp.bfloat16 if a.dtype == jnp.float32 else a.dtype, x),
    )
    start = jax.tree.map(
        lambda part, zero: jnp.broadcast_to(jnp.asarray(zero, part.dtype), part.shape), x, identity
    )

    def turn(k, before):
        at = count - 1 - k
        reached = at > here
        new = combine(
            before, jax.tree.map(lambda part, own: part[at].astype(own.dtype), everything, x)
        )
        return jax.tree.map(lambda a, b: jnp.where(reached, a, b), new, before)

    return lax.fori_loop(0, count, turn, start)


def clip_start(clip_lengths, positions):
    clip_ends = jnp.cumsum(clip_lengths)
    finished = clip_ends[None, :] <= positions[:, None]
    return jnp.sum(jnp.where(finished, clip_lengths[None, :], 0), axis=1)


def column_delays(delay_offsets, columns, group_width):
    codebook = columns // group_width
    matches = codebook[:, None] == jnp.arange(delay_offsets.shape[0], dtype=jnp.int32)[None, :]
    return jnp.sum(jnp.where(matches, delay_offsets[None, :], 0), axis=1)


def prepare(q_raw, k_raw, logit, rate_cap):
    query_rows = q_raw / jnp.sqrt(jnp.sum(q_raw * q_raw, axis=-1, keepdims=True) + EPSILON)
    key_rows = k_raw / jnp.sqrt(jnp.sum(k_raw * k_raw, axis=-1, keepdims=True) + EPSILON)
    beta_rate = rate_cap * jax.nn.sigmoid(logit[:, 0])
    return (query_rows, key_rows, beta_rate)


def span_terms(key_rows, value_rows, beta_rate, clip_begin, span_first):
    span_len = key_rows.shape[0]
    key_width = key_rows.shape[1]
    same_clip = (clip_begin[:, None] == clip_begin[None, :]).astype(jnp.float32)
    gram = beta_rate[:, None] * jnp.dot(key_rows, key_rows.T, precision=HIGHEST) * same_clip
    system = jnp.eye(span_len, dtype=jnp.float32) + jnp.tril(gram, -1)
    stacked = beta_rate[:, None] * jnp.concatenate([key_rows, value_rows], axis=1)
    solved = jax.scipy.linalg.solve_triangular(system, stacked, lower=True, unit_diagonal=True)
    carried = (clip_begin < span_first).astype(jnp.float32)
    final_mask = (clip_begin == clip_begin[-1]).astype(jnp.float32)
    return (solved[:, :key_width], solved[:, key_width:], carried, final_mask, same_clip)


def span_output(state_in, pieces):
    query_rows, key_rows, value_rows, beta_rate, clip_begin, span_first = pieces
    key_part, value_part, carried, final_mask, same_clip = span_terms(
        key_rows, value_rows, beta_rate, clip_begin, span_first
    )
    refreshed = value_part - carried[:, None] * jnp.dot(key_part, state_in, precision=HIGHEST)
    scores = jnp.tril(jnp.dot(query_rows, key_rows.T, precision=HIGHEST)) * same_clip
    outputs = carried[:, None] * jnp.dot(query_rows, state_in, precision=HIGHEST) + jnp.dot(
        scores, refreshed, precision=HIGHEST
    )
    state_out = carried[-1] * state_in + jnp.dot(
        key_rows.T, final_mask[:, None] * refreshed, precision=HIGHEST
    )
    return (state_out, outputs)


def affine_step(affine, pieces):
    key_rows, value_rows, beta_rate, clip_begin, span_first = pieces
    key_part, value_part, carried, final_mask, same_clip = span_terms(
        key_rows, value_rows, beta_rate, clip_begin, span_first
    )
    widened = jnp.concatenate(
        [jnp.zeros((key_rows.shape[0], key_rows.shape[1]), jnp.float32), value_part], axis=1
    )
    refreshed = widened - carried[:, None] * jnp.dot(key_part, affine, precision=HIGHEST)
    return (
        carried[-1] * affine
        + jnp.dot(key_rows.T, final_mask[:, None] * refreshed, precision=HIGHEST),
        None,
    )


def run_head(q_raw, k_raw, v_raw, logit, rate_cap, out_gain, clip_begin, positions, state_in):
    query_rows, key_rows, beta_rate = prepare(q_raw, k_raw, logit, rate_cap)
    span_count = q_raw.shape[0] // SPAN
    pieces = (
        query_rows.reshape(span_count, SPAN, -1),
        key_rows.reshape(span_count, SPAN, -1),
        v_raw.reshape(span_count, SPAN, -1),
        beta_rate.reshape(span_count, SPAN),
        clip_begin.reshape(span_count, SPAN),
        positions.reshape(span_count, SPAN)[:, 0],
    )
    state_out, outputs = lax.scan(span_output, state_in, pieces)
    raw_out = outputs.reshape(-1, outputs.shape[-1])
    normed = (
        raw_out
        / jnp.sqrt(jnp.mean(raw_out * raw_out, axis=-1, keepdims=True) + EPSILON)
        * out_gain[None, :]
    )
    return (normed, state_out)


def compose(before_map, after_map):
    return (
        jnp.matmul(after_map[0], before_map[0], precision=HIGHEST),
        jnp.matmul(after_map[0], before_map[1], precision=HIGHEST) + after_map[1],
    )


def back_product(gradient, weight):
    return lax.dot_general(
        gradient, weight, (((1,), (1,)), ((), ())), preferred_element_type=jnp.float32
    )


def split_heads(matrix, heads_local):
    return matrix.reshape(matrix.shape[0], heads_local, -1).transpose(1, 0, 2)


def join_heads(stacked):
    return stacked.transpose(1, 0, 2).reshape(stacked.shape[1], -1)


def on_device(
    loaded,
    out_grad,
    w_query,
    w_key,
    w_value,
    w_beta,
    beta_max,
    out_gain,
    clip_lengths,
    delay_offsets,
    block_order,
):
    sources = lax.axis_size("seq")
    frames = loaded.shape[0]
    local_width = loaded.shape[1]
    block_rows = frames // sources
    received = lax.all_to_all(
        loaded.reshape(sources, block_rows, local_width),
        "seq",
        split_axis=0,
        concat_axis=0,
        tiled=True,
    )
    inverse = jnp.argsort(block_order[0])
    arranged = jnp.take(received, inverse, axis=0).reshape(frames, local_width)
    positions = lax.axis_index("seq") * frames + jnp.arange(frames, dtype=jnp.int32)
    clip_begin = clip_start(clip_lengths, positions)
    codebooks = delay_offsets.shape[0]
    delay_reach = codebooks - 1
    full_width = local_width * lax.axis_size("head")
    columns = lax.axis_index("head") * local_width + jnp.arange(local_width, dtype=jnp.int32)
    col_delay = column_delays(delay_offsets, columns, full_width // codebooks)
    earlier = from_behind(arranged[frames - delay_reach :], "seq", 1)
    extended = jnp.concatenate([earlier, arranged], axis=0)
    delayed = jnp.zeros((frames, local_width), jnp.bfloat16)
    for shift_by in range(codebooks):
        shifted = extended[delay_reach - shift_by : delay_reach - shift_by + frames]
        inside = positions - shift_by >= clip_begin
        delayed = jnp.where((col_delay[None, :] == shift_by) & inside[:, None], shifted, delayed)
    heads_local = w_beta.shape[1]
    key_width = w_query.shape[1] // heads_local
    value_width = w_value.shape[1] // heads_local
    empty = (
        jnp.zeros((frames, w_query.shape[1]), jnp.float32),
        jnp.zeros((frames, w_key.shape[1]), jnp.float32),
        jnp.zeros((frames, w_value.shape[1]), jnp.float32),
        jnp.zeros((frames, heads_local), jnp.float32),
    )
    feature_part = lax.all_gather(delayed, "head", axis=1, tiled=True)
    results = []
    for running, weight in zip(empty, (w_query, w_key, w_value, w_beta)):
        results.append(jnp.dot(feature_part, weight, preferred_element_type=jnp.float32))
    q_flat, k_flat, v_flat, logit_flat = tuple(results)
    q_heads = split_heads(q_flat, heads_local)
    k_heads = split_heads(k_flat, heads_local)
    v_heads = split_heads(v_flat, heads_local)
    logit_heads = split_heads(logit_flat, heads_local)
    span_count = frames // SPAN
    start_affine = jnp.concatenate(
        [jnp.eye(key_width, dtype=jnp.float32), jnp.zeros((key_width, value_width), jnp.float32)],
        axis=1,
    )

    def head_affine(q_one, k_one, v_one, logit_one, rate_cap):
        query_rows, key_rows, beta_rate = prepare(q_one, k_one, logit_one, rate_cap)
        map_pieces = (
            key_rows.reshape(span_count, SPAN, -1),
            v_one.reshape(span_count, SPAN, -1),
            beta_rate.reshape(span_count, SPAN),
            clip_begin.reshape(span_count, SPAN),
            positions.reshape(span_count, SPAN)[:, 0],
        )
        affine, _ = lax.scan(affine_step, start_affine, map_pieces)
        return affine

    affine = jax.vmap(head_affine)(q_heads, k_heads, v_heads, logit_heads, beta_max)
    transition = affine[:, :, :key_width]
    offset_map = affine[:, :, key_width:]
    identity = (
        jnp.broadcast_to(
            jnp.eye(key_width, dtype=jnp.float32), (heads_local, key_width, key_width)
        ),
        jnp.zeros((heads_local, key_width, value_width), jnp.float32),
    )
    _, state_in = prefix((transition, offset_map), "seq", compose, identity)

    def forward(query_in, key_in, value_in, logit_in, state_start):

        def one_head(q_one, k_one, v_one, logit_one, rate_cap, state_one):
            return run_head(
                q_one, k_one, v_one, logit_one, rate_cap, out_gain, clip_begin, positions, state_one
            )

        return jax.vmap(one_head)(query_in, key_in, value_in, logit_in, beta_max, state_start)

    (normed, state_out), pullback = jax.vjp(
        forward, q_heads, k_heads, v_heads, logit_heads, state_in
    )
    head_out = join_heads(normed).astype(jnp.bfloat16)
    cotangent = split_heads(out_grad, heads_local).astype(jnp.float32)
    first_pass = pullback((cotangent, jnp.zeros_like(state_out)))
    _, state_grad = prefix_2(
        (jnp.swapaxes(transition, 1, 2), first_pass[4]), "seq", compose, identity
    )
    second_pass = pullback((jnp.zeros_like(normed), state_grad))
    gradients = [
        join_heads(first_pass[index] + second_pass[index]).astype(jnp.bfloat16)
        for index in range(4)
    ]
    partial_sum = back_product(gradients[0], w_query) + back_product(gradients[1], w_key)
    partial_sum = (
        partial_sum + back_product(gradients[2], w_value) + back_product(gradients[3], w_beta)
    )
    summed = lax.psum_scatter(
        partial_sum.astype(jnp.bfloat16), "head", scatter_dimension=1, tiled=True
    )
    following = from_behind(summed[:delay_reach], "seq", -1)
    extended_grad = jnp.concatenate([summed, following], axis=0)
    input_grad = jnp.zeros((frames, local_width), jnp.bfloat16)
    for shift_by in range(codebooks):
        ahead = extended_grad[shift_by : shift_by + frames]
        inside = clip_start(clip_lengths, positions + shift_by) <= positions
        input_grad = jnp.where(
            (col_delay[None, :] == shift_by) & inside[:, None], ahead, input_grad
        )
    return (head_out, input_grad)


def solution(mesh):
    return jax.shard_map(
        on_device,
        mesh=mesh,
        in_specs=(
            P("seq", "head"),
            P("seq", "head"),
            P(None, "head"),
            P(None, "head"),
            P(None, "head"),
            P(None, "head"),
            P("head"),
            P(),
            P(),
            P(),
            P("seq", None),
        ),
        out_specs=(P("seq", "head"), P("seq", "head")),
        check_vma=False,
    )
```

profile of v0, /device:TPU:1, one launch (start us, length us, event | category | flops | bytes accessed | tf_op | source)
XLA Modules:
  0.0 574.0 jit_solution(4794235348666533601)
XLA Ops:
  7.2 1.6 reshape.670
  8.9 14.8 %all-to-all-start = ((bf16[64,2,256]{2,1,0:T(2,128)(2,1)}), bf16[64,2,256]{2,1,0:T(2,128)(2,1)S(1)}, u32[]{:S(2)}, u32[]{:S(2)}) async-start(bf16[64,2,256]{2,1,0:T(2,128)(2,1)} %reshape.670), calls=%async_computation | async-start | bytes 131072 | tf_op jit(solution)/shard_map/all_to_all | solution.py:184
  23.8 2.7 sort.17
  27.4 1.3 select_reduce_fusion.2
  30.8 1.9 fusion.106
  35.1 3.5 collective-permute-start
  39.5 21.1 %all_gather.27 = bf16[128,2048]{1,0:T(8,128)(2,1)S(1)} all-gather(bf16[128,256]{1,0:T(8,128)(2,1)S(1)} %and_select_fusion.7), channel_id=1, replica_groups=mesh['seq'=64,'head'=8] {'head'}, dimensions={1}, use_global_device_ids=true | all-gather | bytes 589824 | tf_op jit(solution)/shard_map/all_gather | solution.py:216
  60.7 1.8 multiply_reduce_fusion.10
  64.9 19.7 %custom-call.10 = f32[2,1,128,128]{2,3,1,0:T(8,128)S(1)} custom-call(f32[2,1,128,128]{3,2,1,0:T(8,128)S(1)} %add_bitcast_fusion), custom_call_target="InvertDiagBlocksLowerTriangular" | custom-call | tf_op jit(solution)/shard_map/vmap()/while/body/eval_jaxpr/jit(_solve_triangular)/triangular_solve/custom-call.1 | solution.py:87
  90.5 1.6 copy.156
  94.4 87.9 %all-gather.9.cloned.1.call-done = bf16[128,128,128]{2,1,0:T(8,128)(2,1)} async-done(((bf16[2,128,128]{2,1,0:T(8,128)(2,1)}), bf16[128,128,128]{2,1,0:T(8,128)(2,1)}) %all-gather.9.cloned.1.call-update) | async-done | bytes 4194320 | tf_op jit(solution)/shard_map/all_gather | solution.py:22
  182.3 85.9 %all-gather.11.cloned.1.call-done = bf16[128,128,128]{2,1,0:T(8,128)(2,1)} async-done(((bf16[2,128,128]{2,1,0:T(8,128)(2,1)}), bf16[128,128,128]{2,1,0:T(8,128)(2,1)}) %all-gather.11.cloned.1.call-update) | async-done | bytes 4194320 | tf_op jit(solution)/shard_map/all_gather | solution.py:22
  268.3 1.1 while.25
  275.7 1.1 fusion.63
  278.9 74.5 %all-gather.13.cloned.1.call-done = bf16[128,128,128]{2,1,0:T(8,128)(2,1)} async-done(((bf16[2,128,128]{2,1,0:T(8,128)(2,1)}), bf16[128,128,128]{2,1,0:T(8,128)(2,1)}) %all-gather.13.cloned.1.call-update) | async-done | bytes 4194320 | tf_op jit(solution)/shard_map/all_gather | solution.py:42
  353.4 86.0 %all-gather.15.cloned.1.call-done = bf16[128,128,128]{2,1,0:T(8,128)(2,1)} async-done(((bf16[2,128,128]{2,1,0:T(8,128)(2,1)}), bf16[128,128,128]{2,1,0:T(8,128)(2,1)}) %all-gather.15.cloned.1.call-update) | async-done | bytes 4194320 | tf_op jit(solution)/shard_map/all_gather | solution.py:42
  439.4 73.4 %while.26 = (s32[]{:T(128)}, f32[2,128,128]{2,1,0:T(8,128)S(1)}, s32[]{:T(128)}, bf16[64,2,128,128]{3,2,1,0:T(8,128)(2,1)}, bf16[64,2,128,128]{3,2,1,0:T(8,128)(...) while((s32[]{:T(128)}, f32[2,128,128]{2,1,0:T(8,128)S(1)}, s32[]{:T(128)}, ...), condition=%wide.region_16.19_spmd.clone, body=%wide.region_15.18_spmd.clone.sunk | while | flops 50495496 | bytes 789149 | solution.py:58
  513.3 1.4 convolution_add_fusion.8
  516.7 1.7 multiply_reduce_fusion.1
  522.9 1.2 fusion.11
  525.2 30.1 %reduce-scatter.2.cloned.1.call-done = bf16[128,256]{1,0:T(8,128)(2,1)} async-done(((bf16[128,2048]{1,0:T(8,128)(2,1)}), bf16[128,256]{1,0:T(8,128)(2,1)}) %reduce-scatter.2.cloned.1.call-update) | async-done | bytes 65552 | tf_op jit(solution)/shard_map/reduce_scatter | solution.py:281
  556.0 7.5 %collective-permute-start.1 = (bf16[3,256]{1,0:T(4,128)(2,1)S(1)}, bf16[3,256]{1,0:T(4,128)(2,1)S(1)}, u32[]{:S(2)}, u32[]{:S(2)}) collective-permute-start(bf16[3,256]{1,0:T(4,128)(2,1)S(1)} %slice.115), channel_id=1, source_target_pairs={{8,0},{16,8},{24,16},{32,24},{40,32},{48,40},{56,48},{64,56},{72,6... | collective-permute-start | bytes 4616 | tf_op jit(solution)/shard_map/ppermute | solution.py:16
  564.3 1.5 collective-permute-done.1
  565.9 1.6 and_select_fusion.3
  (337 shorter events, 105.1 us)
Async XLA Ops:
  7.2 85.9 %copy-start = (bf16[2048,256]{1,0:T(8,128)(2,1)S(1)}, bf16[2048,256]{1,0:T(8,128)(2,1)}, u32[]{:S(2)}) copy-start(bf16[2048,256]{1,0:T(8,128)(2,1)} %param.23) | copy-start | bytes 3145732
  7.2 56.3 %copy-start.27 = (bf16[2048,2]{0,1:T(2,128)(2,1)S(1)}, bf16[2048,2]{0,1:T(2,128)(2,1)}, u32[]{:S(2)}) copy-start(bf16[2048,2]{0,1:T(2,128)(2,1)} %param.26) | copy-start | bytes 24580
  7.2 56.3 %copy-start.44 = (f32[2]{0:T(128)S(1)}, f32[2]{0:T(128)}, u32[]{:S(2)}) copy-start(f32[2]{0:T(128)} %param.27) | copy-start | bytes 28
  7.2 77.4 %copy-start.2 = (bf16[2048,256]{1,0:T(8,128)(2,1)S(1)}, bf16[2048,256]{1,0:T(8,128)(2,1)}, u32[]{:S(2)}) copy-start(bf16[2048,256]{1,0:T(8,128)(2,1)} %param.25) | copy-start | bytes 3145732
  8.9 25.4 %all-to-all-start = ((bf16[64,2,256]{2,1,0:T(2,128)(2,1)}), bf16[64,2,256]{2,1,0:T(2,128)(2,1)S(1)}, u32[]{:S(2)}, u32[]{:S(2)}) async-start(bf16[64,2,256]{2,1,0:T(2,128)(2,1)} %reshape.670), calls=%async_computation | async-start | bytes 131072 | tf_op jit(solution)/shard_map/all_to_all | solution.py:184
  23.7 158.6 %all-gather.9.cloned.1.call-start = ((), (), s32[]{:S(2)}) async-start(), calls=%async_computation.3 | async-start | bytes 4259840 | tf_op jit(solution)/shard_map/all_gather | solution.py:22
  30.7 33.6 %copy-start.31 = (pred[256]{0:T(512)(128)(4,1)}, pred[256]{0:T(512)(128)(4,1)S(1)}, u32[]{:S(2)}) copy-start(pred[256]{0:T(512)(128)(4,1)S(1)} %get-tuple-element.999) | copy-start | bytes 772
  30.7 33.6 %copy-start.33 = (pred[256]{0:T(512)(128)(4,1)}, pred[256]{0:T(512)(128)(4,1)S(1)}, u32[]{:S(2)}) copy-start(pred[256]{0:T(512)(128)(4,1)S(1)} %get-tuple-element.1000) | copy-start | bytes 772
  35.1 4.3 collective-permute-start
  39.5 52.6 %copy-start.16 = (bf16[128,256]{1,0:T(8,128)(2,1)S(1)}, bf16[128,256]{1,0:T(8,128)(2,1)}, u32[]{:S(2)}) copy-start(bf16[128,256]{1,0:T(8,128)(2,1)} %param.22) | copy-start | bytes 196612
  88.0 181.5 %copy-start.21 = (f32[128]{0:T(128)S(1)}, f32[128]{0:T(128)}, u32[]{:S(2)}) copy-start(f32[128]{0:T(128)} %copy-done.20) | copy-start | bytes 1540
  89.7 178.6 %all-gather.11.cloned.1.call-start = ((), (), s32[]{:S(2)}) async-start(), calls=%async_computation.4 | async-start | bytes 4259840 | tf_op jit(solution)/shard_map/all_gather | solution.py:22
  90.4 263.0 %all-gather.13.cloned.1.call-start = ((), (), s32[]{:S(2)}) async-start(), calls=%async_computation.5 | async-start | bytes 4259840 | tf_op jit(solution)/shard_map/all_gather | solution.py:42
  92.0 347.4 %all-gather.15.cloned.1.call-start = ((), (), s32[]{:S(2)}) async-start(), calls=%async_computation.6 | async-start | bytes 4259840 | tf_op jit(solution)/shard_map/all_gather | solution.py:42
  94.4 179.9 %copy-start.15 = (f32[2,128,128]{2,1,0:T(8,128)}, f32[2,128,128]{2,1,0:T(8,128)S(1)}, u32[]{:S(2)}) copy-start(f32[2,128,128]{2,1,0:T(8,128)S(1)} %fusion.25) | copy-start | bytes 393220
  272.7 282.6 %reduce-scatter.2.cloned.1.call-start = ((), (), s32[]{:S(2)}) async-start(), calls=%async_computation.2 | async-start | bytes 589824 | tf_op jit(solution)/shard_map/reduce_scatter | solution.py:281
  276.8 237.9 %copy-start.22 = (f32[128]{0:T(128)S(1)}, f32[128]{0:T(128)}, u32[]{:S(2)}) copy-start(f32[128]{0:T(128)} %copy-done.20) | copy-start | bytes 1540
  278.4 238.3 %copy-start.24 = (f32[2,128]{1,0:T(2,128)S(1)}, f32[2,128]{1,0:T(2,128)}, u32[]{:S(2)}) copy-start(f32[2,128]{1,0:T(2,128)} %copy-done.23) | copy-start | bytes 3076
  521.8 44.0 %copy-start.32 = (pred[256]{0:T(512)(128)(4,1)S(1)}, pred[256]{0:T(512)(128)(4,1)}, u32[]{:S(2)}) copy-start(pred[256]{0:T(512)(128)(4,1)} %copy-done.31) | copy-start | bytes 772
  521.8 44.0 %copy-start.34 = (pred[256]{0:T(512)(128)(4,1)S(1)}, pred[256]{0:T(512)(128)(4,1)}, u32[]{:S(2)}) copy-start(pred[256]{0:T(512)(128)(4,1)} %copy-done.33) | copy-start | bytes 772
  521.8 44.0 %copy-start.36 = (pred[256]{0:T(512)(128)(4,1)S(1)}, pred[256]{0:T(512)(128)(4,1)}, u32[]{:S(2)}) copy-start(pred[256]{0:T(512)(128)(4,1)} %copy-done.35) | copy-start | bytes 772
  521.8 44.0 %copy-start.38 = (pred[256]{0:T(512)(128)(4,1)S(1)}, pred[256]{0:T(512)(128)(4,1)}, u32[]{:S(2)}) copy-start(pred[256]{0:T(512)(128)(4,1)} %copy-done.37) | copy-start | bytes 772
  521.9 44.0 %copy-start.41 = (pred[128]{0:T(512)(128)(4,1)S(1)}, pred[128]{0:T(512)(128)(4,1)}, u32[]{:S(2)}) copy-start(pred[128]{0:T(512)(128)(4,1)} %get-tuple-element.1003) | copy-start | bytes 388
  556.0 9.8 %collective-permute-start.1 = (bf16[3,256]{1,0:T(4,128)(2,1)S(1)}, bf16[3,256]{1,0:T(4,128)(2,1)S(1)}, u32[]{:S(2)}, u32[]{:S(2)}) collective-permute-start(bf16[3,256]{1,0:T(4,128)(2,1)S(1)} %slice.115), channel_id=1, source_target_pairs={{8,0},{16,8},{24,16},{32,24},{40,32},{48,40},{56,48},{64,56},{72,6... | collective-permute-start | bytes 4616 | tf_op jit(solution)/shard_map/ppermute | solution.py:16
  (33 other events, 219.8 us)
Sparse Core Ops, SparseCore 0:
  89.8 92.4 all-gather.8
  186.3 81.9 all-gather.10
  271.6 81.7 all-gather.12
  357.2 82.2 all-gather.14
  524.3 31.0 reduce-scatter.1
where the time goes:
time: 581 us; the launch traced here: 574 us
  waiting for transfers between devices  367 us (63%)
  matrix products  98.1 us (17%)
  other arithmetic  30.5 us (5%)
  starting transfers between devices  26.2 us (5%)
  blocking collectives  21.1 us (4%)
  between operations  15.6 us (3%)
  local copies, waits for them, and re-layouts  12.1 us (2%)
    all_gather x2, waiting for transfers between devices, prefix(): lax.all_gather(a.astype(kind), axis)  174 us
    all_gather x2, waiting for transfers between devices, prefix_2(): lax.all_gather(part.astype(kind), axis)  161 us
    dot_general x65, matrix products, compose(): jnp.matmul(after_map[0], before_map[1], precision=HIGHEST) + after_map[1]  71 us
    reduce_scatter x1, waiting for transfers between devices, on_device(): lax.psum_scatter(partial_sum.astype(jnp.bfloat16), 'head', scatter_dimens...  30.1 us
    all_gather x1, blocking collectives, on_device(): feature_part = lax.all_gather(delayed, 'head', axis=1, tiled=True)  21.1 us
    another operation x5, other arithmetic, span_terms(): jax.scipy.linalg.solve_triangular(system, stacked, lower=True, unit_diago...  19.9 us
    all_to_all x1, starting transfers between devices, on_device(): lax.all_to_all(loaded.reshape(sources, block_rows, local_width), 'seq', s...  14.8 us
  transfers between devices with their start and end apart: 8, of which 7 were waited for; matrix products, arithmetic and copies ran while one was open for 4% of the time, Pallas kernels for 0%

commit v1 on v0

v1 whole, which is shorter than its diff:
```python
import functools

import jax
import jax.numpy as jnp
from jax import lax
from jax.experimental import pallas as pl
from jax.experimental.pallas import tpu as pltpu
from jax.sharding import PartitionSpec as P

EPSILON = 1e-06
F32, BF16 = jnp.float32, jnp.bfloat16
CORES = 2
CHIPS_X = 4

NN = (1, 0)
NT = (1, 1)
TN = (0, 0)


def dot(a, b, kind=NN):
    return lax.dot_general(
        a, b, (((kind[0],), (kind[1],)), ((), ())), preferred_element_type=F32
    )


def split(x):
    high = x.astype(BF16)
    return high, (x - high.astype(F32)).astype(BF16)


def mm3(a, b, kind=NN):
    ah, al = split(a)
    bh, bl = split(b)
    return dot(
        jnp.concatenate([ah, ah, al], axis=kind[0]),
        jnp.concatenate([bh, bl, bh], axis=kind[1]),
        kind,
    )


def mm2(a, b, kind=NN):
    bh, bl = split(b)
    return dot(
        jnp.concatenate([a, a], axis=kind[0]), jnp.concatenate([bh, bl], axis=kind[1]), kind
    )


def mm1(a, b, kind=NN):
    return dot(a.astype(BF16), b.astype(BF16), kind)


def one_hot(condition):
    return jnp.where(condition, 1.0, 0.0).astype(BF16)


def iota(shape, dim):
    return lax.broadcasted_iota(jnp.int32, shape, dim)


def clip_start(lengths, positions):
    begin = jnp.zeros_like(positions)
    end = jnp.int32(0)
    for c in range(lengths.shape[0]):
        size = lengths[c]
        end = end + size
        begin = begin + jnp.where(end <= positions, size, 0)
    return begin


def kernel(
    dims,
    loaded,
    out_grad,
    w_query,
    w_key,
    w_value,
    w_beta,
    beta_max,
    out_gain,
    clip_lengths,
    delay_offsets,
    block_order,
    head_out,
    input_grad,
    wq,
    wk,
    wv,
    cot,
    r1,
    s2,
    r2,
    arranged,
    tail,
    feat,
    acc,
    ab,
    sib_ab,
    plane,
    group,
    from_z1,
    from_z2,
    a_next,
    states,
    grads,
    sib_grad,
    gplane,
    ggroup,
    gz1,
    gz2,
    dstates,
    gcat,
    rs_send,
    rs_recv,
    summed,
    follow,
    give_s,
    give_d,
    local_sem,
    send_sem,
    recv_sem,
):
    Z, X, H, F, W = dims["Z"], dims["X"], dims["H"], dims["F"], dims["W"]
    C = CORES
    G = X * C
    S = Z * G
    BR = F // S
    N = 128
    CB = delay_offsets.shape[0]
    seq, y = lax.axis_index("seq"), lax.axis_index("head")
    z = lax.div(seq, G)
    g = lax.rem(seq, G)
    x = lax.div(g, C)
    core = lax.rem(g, C)
    other = 1 - core

    def at(zz, gg):
        return (zz * G + gg, y)

    counter = [0]
    started = []

    def remote(src, dst, device, index=None):
        if index is None:
            index = counter[0]
            counter[0] += 1
        return pltpu.make_async_remote_copy(
            src_ref=src,
            dst_ref=dst,
            send_sem=send_sem.at[index],
            recv_sem=recv_sem.at[index],
            device_id=device,
            device_id_type=pl.DeviceIdType.MESH,
        )

    def go(copy):
        copy.start()
        started.append(copy)
        return copy

    fetches = [
        pltpu.make_async_copy(src, dst, local_sem.at[i])
        for i, (src, dst) in enumerate(
            ((w_query, wq), (w_key, wk), (w_value, wv), (out_grad, cot))
        )
    ]
    for copy in fetches:
        copy.start()

    partners = [at(lax.rem(z + k, Z), g) for k in range(1, Z)]
    partners += [at(z, lax.rem(g + k, G)) for k in range(1, G)]
    partners += [(lax.rem(seq + 1, S), y), (lax.rem(seq + S - 1, S), y)]
    partners += [(seq, lax.rem(y + 1, H)), (seq, lax.rem(y + H - 1, H))]
    barrier = pltpu.get_barrier_semaphore()
    for partner in partners:
        pl.semaphore_signal(barrier, inc=1, device_id=partner, device_id_type=pl.DeviceIdType.MESH)
    pl.semaphore_wait(barrier, len(partners))

    rows1 = G * BR
    copies = []
    for k in range(1, Z):
        to = lax.rem(z + k, Z)
        src = loaded.at[pl.ds(pl.multiple_of(to * rows1, rows1), rows1)]
        copies.append(go(remote(src, r1.at[z], at(to, g))))
    r1[z] = loaded[pl.ds(pl.multiple_of(z * rows1, rows1), rows1), :]

    first = seq * F
    pos_col = first + iota((F, 1), 0)
    begin_col = clip_start(clip_lengths, pos_col)
    begin_row = clip_start(clip_lengths, first + iota((1, F), 1))
    delay = delay_offsets[lax.div(y * CB, H)]
    row, col = iota((F, F), 0), iota((F, F), 1)
    same = jnp.where(begin_col == begin_row, 1.0, 0.0)
    low = jnp.where(row > col, same, 0.0)
    low_eq = jnp.where(row >= col, same, 0.0)
    eye = jnp.where(row == col, 1.0, 0.0)
    carried = jnp.where(begin_col < first, 1.0, 0.0)
    final = jnp.where(begin_col == begin_col[F - 1 : F, :], 1.0, 0.0)
    carried_last = carried[F - 1 : F, :]

    zbr = Z * BR
    to_g, to_z, to_r = row // zbr, (row % zbr) // BR, row % BR
    regroup = one_hot(col == to_z * rows1 + to_g * BR + to_r)
    order = jnp.broadcast_to(block_order[...], (16, S)).astype(F32).astype(BF16)
    src_i, out_q = iota((S, F), 0), iota((S, F), 1)
    spread = one_hot(src_i == ((out_q % zbr) // BR) * G + out_q // zbr)
    target = dot(order, spread)[0:1, :].astype(jnp.int32) * BR + iota((1, F), 1) % BR
    place = one_hot(row == target)

    for copy in copies:
        copy.wait_recv()
    s2[...] = dot(regroup, r1[...].reshape(F, W)).astype(BF16).reshape(G, zbr, W)
    copies = []
    for k in range(1, G):
        to = lax.rem(g + k, G)
        copies.append(go(remote(s2.at[to], r2.at[g], at(z, to))))
    r2[g] = s2[g]
    for copy in copies:
        copy.wait_recv()
    arranged[...] = dot(place, r2[...].reshape(F, W)).astype(BF16)

    halo = go(remote(arranged.at[pl.ds(F - 16, 16)], tail, (lax.rem(seq + 1, S), y)))
    half = F // 2
    halves = (half, 0)

    def delayed_rows(start, source_first, source_count):
        frames = first + start + iota((half, 1), 0)
        wanted = jnp.where(frames - delay >= begin_col[start : start + half, :], frames - delay, -100)
        return one_hot(wanted == first + source_first + iota((half, source_count), 1))

    up, down = (seq, lax.rem(y + 1, H)), (seq, lax.rem(y + H - 1, H))
    hops = (H // 2, H - 1 - H // 2)
    sign = (-1, 1)
    gathers = {}
    for d in range(2):
        for s in range(hops[d]):
            for b in range(2):
                owner = lax.rem(y + sign[d] * s + H, H)
                part = feat.at[owner, pl.ds(halves[b], half)]
                gathers[d, s, b] = remote(part, part, (up, down)[d])

    feat[y, half:F, :] = dot(delayed_rows(half, 0, F), arranged[...]).astype(BF16)
    for d in range(2):
        if hops[d]:
            go(gathers[d, 0, 0])
    halo.wait_recv()
    both = jnp.concatenate([tail[...], arranged[...]], axis=0)
    feat[y, 0:half, :] = dot(delayed_rows(0, -16, F + 16), both).astype(BF16)
    for d in range(2):
        if hops[d]:
            go(gathers[d, 0, 1])

    def project(owner, begin):
        block = feat[owner]
        here = pl.ds(pl.multiple_of(owner * W, W), W)
        for i, weight in enumerate((wq, wk, wv)):
            value = dot(block, weight[here, :])
            at_cols = slice(i * W, (i + 1) * W)
            acc[:, at_cols] = value if begin else acc[:, at_cols] + value
        value = dot(block, w_beta[:, here], NT)
        acc[:, 3 * W : 3 * W + 16] = value if begin else acc[:, 3 * W : 3 * W + 16] + value

    for copy in fetches:
        copy.wait()
    project(y, True)
    for s in range(hops[0]):
        for b in range(2):
            for d in range(2):
                if s < hops[d]:
                    gathers[d, s, b].wait_recv()
                    if s + 1 < hops[d]:
                        go(gathers[d, s + 1, b])
        for d in range(2):
            if s < hops[d]:
                project(lax.rem(y + sign[d] * (s + 1) + H, H), False)

    heads = range(2)
    Q, K, V, beta, nq, nk, sig, Gm, T = ({} for _ in range(9))
    for h in heads:
        cols = slice(h * N, (h + 1) * N)
        q_raw, k_raw = acc[:, cols], acc[:, W + h * N : W + (h + 1) * N]
        V[h] = acc[:, 2 * W + h * N : 2 * W + (h + 1) * N]
        nq[h] = lax.rsqrt(jnp.sum(q_raw * q_raw, axis=1, keepdims=True) + EPSILON)
        nk[h] = lax.rsqrt(jnp.sum(k_raw * k_raw, axis=1, keepdims=True) + EPSILON)
        Q[h], K[h] = q_raw * nq[h], k_raw * nk[h]
        sig[h] = 1.0 / (1.0 + jnp.exp(-acc[:, 3 * W + h : 3 * W + h + 1]))
        beta[h] = beta_max[h] * sig[h]
    L = {}
    for h in heads:
        Gm[h] = mm3(K[h], K[h], NT) * low
        L[h] = beta[h] * Gm[h]
    size = 1
    while size < F:
        pair = (
            ((row // (2 * size)) == (col // (2 * size)))
            & ((row // size) % 2 == 1)
            & ((col // size) % 2 == 0)
        )
        inner = {h: jnp.where(pair, L[h], 0.0) for h in heads}
        if size == 1:
            T = {h: eye - inner[h] for h in heads}
        else:
            half_way = {h: mm3(T[h], inner[h]) for h in heads}
            T = {h: T[h] - mm3(half_way[h], T[h]) for h in heads}
        size *= 2
    Wk, Wv = {}, {}
    for h in heads:
        both = mm3(T[h], beta[h] * jnp.concatenate([K[h], V[h]], axis=1))
        Wk[h], Wv[h] = both[:, :N], both[:, N:]
    for h in heads:
        both = mm3(K[h], jnp.concatenate([Wk[h], final * Wv[h]], axis=1), TN)
        ab[h, :, :N] = carried_last * (eye - both[:, :N])
        ab[h, :, N:] = both[:, N:]

    sibling = at(z, x * C + other)
    copy = go(remote(ab.at[other], sib_ab, sibling))
    P_, Oloc, R = {}, {}, {}
    for h in heads:
        P_[h] = mm3(Q[h], K[h], NT) * low_eq
        both = mm3(P_[h], jnp.concatenate([carried * Wk[h], Wv[h]], axis=1))
        R[h] = carried * Q[h] - both[:, :N]
        Oloc[h] = both[:, N:]
    copy.wait_recv()
    own, sib = ab[core], sib_ab[...]
    early = jnp.where(core == 0, own, sib)
    late = jnp.where(core == 0, sib, own)
    a_early, b_early = early[:, :N], early[:, N:]
    a_late, b_late = late[:, :N], late[:, N:]
    zero = jnp.zeros((N, N), F32)
    pad_b = jnp.concatenate([zero, b_late], axis=1)
    plane[x] = (mm3(a_late, early) + pad_b).astype(BF16)
    copies = []
    for k in range(1, X):
        to = lax.rem(x + k, X)
        copies.append(go(remote(plane.at[x], plane.at[x], at(z, to * C + core))))
    for copy in copies:
        copy.wait_recv()

    def then(before, after):
        shift = jnp.concatenate([zero, after[:, N:].astype(F32)], axis=1)
        return mm2(after[:, :N], before) + shift

    def then32(before, after):
        shift = jnp.concatenate([zero, after[:, N:]], axis=1)
        return mm3(after[:, :N], before) + shift

    maps = [plane[i] for i in range(X)]
    identity = jnp.concatenate([eye, zero], axis=1)
    prefix = [identity, maps[0].astype(F32)]
    if X == 4:
        front = then(prefix[1], maps[1])
        back = then(maps[2].astype(F32), maps[3])
        total = then32(front, back)
        prefix += [front]
    else:
        for i in range(1, X):
            total = then(prefix[-1], maps[i])
            prefix.append(total)
    group[...] = total.astype(BF16)
    z1, z2 = lax.rem(z + 1, Z), lax.rem(z + 2, Z)
    y1, y2 = lax.rem(z + Z - 1, Z), lax.rem(z + Z - 2, Z)
    copies = [
        go(remote(group, from_z1, at(z1, g))),
        go(remote(group.at[:, pl.ds(N, N)], from_z2, at(z2, g))),
    ]
    next_copy = go(remote(group.at[:, pl.ds(0, N)], a_next, at(y1, g)))
    if X == 4:
        prefix.append(then(front, maps[2]))
        a1, a2, a3 = (maps[i][:, :N] for i in (1, 2, 3))
        suffix = [mm2(a3, mm2(a2, a1.astype(F32))), back[:, :N], a3.astype(F32), eye]
    else:
        suffix = [eye]
        for i in range(X - 1, 0, -1):
            suffix.insert(0, mm3(suffix[0], maps[i][:, :N].astype(F32)))

    def pick(options, index):
        value = options[0]
        for i in range(1, len(options)):
            value = jnp.where(index == i, options[i], value)
        return value

    before_me = pick(prefix[:X], x)
    after_me = pick(suffix, x)
    for copy in copies:
        copy.wait_recv()
    s_group = from_z1[:, N:].astype(F32) + dot(from_z1[:, :N], from_z2[...])
    s_chip = before_me[:, N:] + mm3(before_me[:, :N], s_group)
    s_late = b_early + mm3(a_early, s_chip)
    states[core] = jnp.where(core == 0, s_chip, s_late)
    give_s[...] = jnp.where(core == 0, s_late, s_chip)
    go(remote(give_s, states.at[core], sibling)).wait_recv()

    gain = out_gain[...]
    O, dO = {}, {}
    for h in heads:
        cols = slice(h * N, (h + 1) * N)
        O[h] = Oloc[h] + mm3(R[h], states[h])
        inv = lax.rsqrt(jnp.mean(O[h] * O[h], axis=1, keepdims=True) + EPSILON)
        head_out[:, cols] = (O[h] * inv * gain).astype(BF16)
        scaled = cot[:, cols].astype(F32) * gain
        unit = O[h] * inv
        dO[h] = inv * (scaled - unit * jnp.mean(scaled * unit, axis=1, keepdims=True))
        grads[h] = mm3(R[h], dO[h], TN)
    copy = go(remote(grads.at[other], sib_grad, sibling))
    U, dU0, Y, dX0, dP, dQ, dK0, Zv = ({} for _ in range(8))
    for h in heads:
        S0 = states[h]
        KS = carried * mm3(K[h], S0)
        Zv[h] = V[h] - KS
        U[h] = Wv[h] - carried * mm3(Wk[h], S0)
    copy.wait_recv()
    own, sib = grads[core], sib_grad[...]
    g_early = jnp.where(core == 0, own, sib)
    g_late = jnp.where(core == 0, sib, own)
    gplane[x] = (g_early + mm3(a_early, g_late, TN)).astype(BF16)
    copies = []
    for k in range(1, X):
        to = lax.rem(x + k, X)
        copies.append(go(remote(gplane.at[x], gplane.at[x], at(z, to * C + core))))
    for h in heads:
        dU0[h] = mm3(P_[h], dO[h], TN)
        both = mm3(T[h], jnp.concatenate([dU0[h], final * K[h]], axis=1), TN)
        dX0[h], Y[h] = both[:, :N], both[:, N:]
    for copy in copies:
        copy.wait_recv()
    gs = [gplane[i].astype(F32) for i in range(X)]

    def back_through(i, later):
        return gs[i] + mm2(maps[i][:, :N], later, TN)

    if X == 4:
        pair_late = back_through(2, gs[3])
        pair_early = back_through(0, gs[1])
        g_total = pair_early + mm3(front[:, :N], pair_late, TN)
        behind = [back_through(1, pair_late), pair_late, gs[3], zero]
    else:
        behind = [zero]
        for i in range(X - 1, -1, -1):
            behind.insert(0, back_through(i, behind[0]))
        g_total = behind[0]
        behind = behind[1:]
    ggroup[...] = g_total.astype(BF16)
    copies = [
        go(remote(ggroup, gz1, at(y1, g))),
        go(remote(ggroup, gz2, at(y2, g))),
    ]
    behind_me = pick(behind, x)
    for h in heads:
        S0 = states[h]
        dP[h] = mm3(dO[h], U[h], NT) * low_eq
        dQ[h] = carried * mm3(dO[h], S0, NT) + mm3(dP[h], K[h])
        dK0[h] = mm3(dP[h], Q[h], TN)
        grad = nq[h] * (dQ[h] - Q[h] * jnp.sum(Q[h] * dQ[h], axis=1, keepdims=True))
        gcat[:, h * N : (h + 1) * N] = grad.astype(BF16)
    next_copy.wait_recv()
    for copy in copies:
        copy.wait_recv()
    d_group = gz1[...].astype(F32) + dot(a_next[...], gz2[...], TN)
    d_chip = behind_me + mm3(after_me, d_group, TN)
    d_early = g_late + mm3(a_late, d_chip, TN)
    dstates[core] = jnp.where(core == 0, d_early, d_chip)
    give_d[...] = jnp.where(core == 0, d_chip, d_early)
    go(remote(give_d, dstates.at[core], sibling)).wait_recv()

    dlog = jnp.zeros((F, 16), F32)
    for h in heads:
        S0, dS = states[h], dstates[h]
        dX = dX0[h] + mm3(Y[h], dS)
        scaled = beta[h] * dX
        both = mm3(dX, jnp.concatenate([U[h], S0], axis=0), NT)
        dL = -both[:, :F] * low
        dG = beta[h] * dL
        dK = dK0[h] + mm3(final * U[h], dS, NT)
        dK = dK - carried * beta[h] * both[:, F:]
        dK = dK + mm3(dG, K[h]) + mm3(dG, K[h], TN)
        d_beta = jnp.sum(dX * Zv[h], axis=1, keepdims=True)
        d_beta = d_beta + jnp.sum(dL * Gm[h], axis=1, keepdims=True)
        grad = nk[h] * (dK - K[h] * jnp.sum(K[h] * dK, axis=1, keepdims=True))
        gcat[:, W + h * N : W + (h + 1) * N] = grad.astype(BF16)
        gcat[:, 2 * W + h * N : 2 * W + (h + 1) * N] = scaled.astype(BF16)
        d_logit = d_beta * beta[h] * (1.0 - sig[h])
        dlog = dlog + jnp.where(iota((F, 16), 1) == h, d_logit, 0.0)
    dlog = dlog.astype(BF16)

    def partial(owner):
        here = pl.ds(pl.multiple_of(owner * W, W), W)
        value = dot(dlog, w_beta[:, here])
        for i, weight in enumerate((wq, wk, wv)):
            value = value + dot(gcat[:, i * W : (i + 1) * W], weight[here, :], NT)
        return value

    base = (0, hops[0])
    reduces = {}
    for d in range(2):
        for s in range(hops[d]):
            for b in range(2):
                slot = base[d] + s
                reduces[d, s, b] = remote(
                    rs_send.at[slot, b], rs_recv.at[slot, b], (up, down)[d]
                )
    for s in range(hops[0]):
        values = {}
        for d in range(2):
            if s < hops[d]:
                owner = y + hops[0] - s if d == 0 else y - hops[1] + s + H
                values[d] = partial(lax.rem(owner, H))
        for b in range(2):
            for d in range(2):
                if s < hops[d]:
                    slot = base[d] + s
                    value = values[d][b * half : (b + 1) * half, :]
                    if s:
                        reduces[d, s - 1, b].wait_recv()
                        value = value + rs_recv[slot - 1, b].astype(F32)
                    rs_send[slot, b] = value.astype(BF16)
                    go(reduces[d, s, b])
    mine = partial(y)
    for b in range(2):
        value = mine[b * half : (b + 1) * half, :]
        for d in range(2):
            if hops[d]:
                reduces[d, hops[d] - 1, b].wait_recv()
                value = value + rs_recv[base[d] + hops[d] - 1, b].astype(F32)
        summed[b * half : (b + 1) * half, :] = value.astype(BF16)
        if b == 0:
            halo = go(remote(summed.at[pl.ds(0, 16)], follow, (lax.rem(seq + S - 1, S), y)))
    ahead = pos_col + delay
    reaches = (ahead < S * F) & (clip_start(clip_lengths, ahead) <= pos_col)
    wanted = jnp.where(reaches, ahead - first, -1)
    pull = one_hot(wanted == iota((F, F + 16), 1))
    halo.wait_recv()
    both = jnp.concatenate([summed[...], follow[...]], axis=0)
    input_grad[...] = dot(pull, both).astype(BF16)
    for copy in started:
        copy.wait_send()


def on_device(
    dims,
    loaded,
    out_grad,
    w_query,
    w_key,
    w_value,
    w_beta,
    beta_max,
    out_gain,
    clip_lengths,
    delay_offsets,
    block_order,
):
    Z, X, H = dims["Z"], dims["X"], dims["H"]
    F, W = dims["F"], dims["W"]
    G = X * CORES
    BR = F // (Z * G)
    N = 128
    half = F // 2
    hops = H - 1
    count = 128
    vmem, smem, anyw = (
        pl.BlockSpec(memory_space=s) for s in (pltpu.VMEM, pltpu.SMEM, pl.ANY)
    )
    D = w_query.shape[0]
    scratch = [
        pltpu.VMEM((D, W), BF16),
        pltpu.VMEM((D, W), BF16),
        pltpu.VMEM((D, W), BF16),
        pltpu.VMEM((F, W), BF16),
        pltpu.VMEM((Z, G * BR, W), BF16),
        pltpu.VMEM((G, Z * BR, W), BF16),
        pltpu.VMEM((G, Z * BR, W), BF16),
        pltpu.VMEM((F, W), BF16),
        pltpu.VMEM((16, W), BF16),
        pltpu.VMEM((H, F, W), BF16),
        pltpu.VMEM((F, 3 * W + 128), F32),
        pltpu.VMEM((2, N, 2 * N), F32),
        pltpu.VMEM((N, 2 * N), F32),
        pltpu.VMEM((X, N, 2 * N), BF16),
        pltpu.VMEM((N, 2 * N), BF16),
        pltpu.VMEM((N, 2 * N), BF16),
        pltpu.VMEM((N, N), BF16),
        pltpu.VMEM((N, N), BF16),
        pltpu.VMEM((2, N, N), F32),
        pltpu.VMEM((2, N, N), F32),
        pltpu.VMEM((N, N), F32),
        pltpu.VMEM((X, N, N), BF16),
        pltpu.VMEM((N, N), BF16),
        pltpu.VMEM((N, N), BF16),
        pltpu.VMEM((N, N), BF16),
        pltpu.VMEM((2, N, N), F32),
        pltpu.VMEM((F, 3 * W), BF16),
        pltpu.VMEM((hops, 2, half, W), BF16),
        pltpu.VMEM((hops, 2, half, W), BF16),
        pltpu.VMEM((F, W), BF16),
        pltpu.VMEM((16, W), BF16),
        pltpu.VMEM((N, N), F32),
        pltpu.VMEM((N, N), F32),
        pltpu.SemaphoreType.DMA((4,)),
        pltpu.SemaphoreType.DMA((count,)),
        pltpu.SemaphoreType.DMA((count,)),
    ]
    wide_beta = jnp.pad(w_beta.T, ((0, 14), (0, 0)))
    return pl.pallas_call(
        functools.partial(kernel, dims),
        out_shape=(
            jax.ShapeDtypeStruct((F, W), BF16),
            jax.ShapeDtypeStruct((F, W), BF16),
        ),
        in_specs=[vmem, anyw, anyw, anyw, anyw, vmem, smem, vmem, smem, smem, vmem],
        out_specs=(vmem, vmem),
        scratch_shapes=scratch,
        compiler_params=pltpu.CompilerParams(
            collective_id=0, has_side_effects=True, vmem_limit_bytes=40 * 2**20
        ),
    )(
        loaded,
        out_grad,
        w_query,
        w_key,
        w_value,
        wide_beta,
        beta_max,
        out_gain.reshape(1, -1),
        clip_lengths,
        delay_offsets,
        block_order,
    )


def build(mesh, chips_x, frames):
    seq, head = mesh.shape["seq"], mesh.shape["head"]
    dims = dict(Z=seq // (chips_x * CORES), X=chips_x, H=head, F=frames, W=256)
    return jax.shard_map(
        functools.partial(on_device, dims),
        mesh=mesh,
        in_specs=(
            P("seq", "head"),
            P("seq", "head"),
            P(None, "head"),
            P(None, "head"),
            P(None, "head"),
            P(None, "head"),
            P("head"),
            P(),
            P(),
            P(),
            P("seq", None),
        ),
        out_specs=(P("seq", "head"), P("seq", "head")),
        check_vma=False,
    )


def solution(mesh):
    return build(mesh, CHIPS_X, 128)
```

time: 581 us -> 92.2 us (0.16); the launches traced: 574 us -> 91.9 us
  waiting for transfers between devices: 367 us -> 0 us
  matrix products: 98.1 us -> 0 us
  Pallas kernels: 0 us -> 84.6 us
  other arithmetic: 30.5 us -> 0 us
  starting transfers between devices: 26.2 us -> 0 us
  blocking collectives: 21.1 us -> 0 us
  between operations: 15.6 us -> 0.73 us
    all_gather x4 -> x0, waiting for transfers between devices: 334 us -> none  [the longest x2 174 us: prefix(): lax.all_gather(a.astype(kind), axis)]
    dot_general x101 -> x0, matrix products: 91 us -> none  [the longest x65 71 us: compose(): jnp.matmul(after_map[0], before_map[1], precision=HIGHEST) + after_map[1]]
    pallas_call x0 -> x1, Pallas kernels: none -> 84.6 us  [on_device(): pl.pallas_call(functools.partial(kernel, dims), out_shape=(jax.ShapeDtype...]
    reduce_scatter x1 -> x0, waiting for transfers between devices: 30.1 us -> none  [on_device(): lax.psum_scatter(partial_sum.astype(jnp.bfloat16), 'head', scatter_dimens...]
    all_gather x1 -> x0, blocking collectives: 21.1 us -> none  [on_device(): feature_part = lax.all_gather(delayed, 'head', axis=1, tiled=True)]
    another operation x8 -> x0, other arithmetic: 20 us -> none  [the longest x5 19.9 us: span_terms(): jax.scipy.linalg.solve_triangular(system, stacked, lower=True, unit_diago...]
    all_to_all x1 -> x0, starting transfers between devices: 14.8 us -> none  [on_device(): lax.all_to_all(loaded.reshape(sources, block_rows, local_width), 'seq', s...]
    ppermute x2 -> x0, starting transfers between devices: 11 us -> none  [from_behind(): return lax.ppermute(x, axis, pairs)]
  transfers between devices with their start and end apart: 8 -> 0, of which waited for: 7 -> 0; matrix products, arithmetic and copies ran while one was open for 4% -> 0% of each run, Pallas kernels for 0% -> 0%
where the time goes in v1:
time: 92.2 us; the launch traced here: 91.9 us
  Pallas kernels  84.6 us (92%)
  local copies, waits for them, and re-layouts  6.57 us (7%)
    pallas_call x1, Pallas kernels, on_device(): pl.pallas_call(functools.partial(kernel, dims), out_shape=(jax.ShapeDtype...  84.6 us
    unnamed x22, local copies, waits for them, and re-layouts  5.81 us

profile of v1, /device:TPU:1, one launch (start us, length us, event | category | flops | bytes accessed | tf_op | source)
XLA Modules:
  0.0 91.9 jit_solution(6727824156560330270)
XLA Ops:
  0.6 0.0 copy-start.3
  0.6 0.0 copy-start.5
  0.7 0.0 copy-start.6
  0.7 0.0 copy-start.7
  0.7 0.0 copy-start.8
  0.7 0.0 copy-start.9
  0.7 0.8 pad.4.w_beta
  1.5 0.0 copy-done.3
  1.5 0.0 copy-done.5
  1.5 0.0 copy-done.6
  1.5 0.0 copy-done.7
  1.5 0.0 copy-done.8
  1.5 0.0 copy-done.9
  1.5 0.0 copy-start
  1.5 1.2 %copy-done = bf16[2048,256]{1,0:T(8,128)(2,1)S(1)} copy-done((bf16[2048,256]{1,0:T(8,128)(2,1)S(1)}, bf16[2048,256]{1,0:T(8,128)(2,1)}, u32[]{:S(2)}) %copy-start) | copy-done | bytes 1048600
  2.7 0.0 copy-start.1
  2.7 1.2 %copy-done.1 = bf16[2048,256]{1,0:T(8,128)(2,1)S(1)} copy-done((bf16[2048,256]{1,0:T(8,128)(2,1)S(1)}, bf16[2048,256]{1,0:T(8,128)(2,1)}, u32[]{:S(2)}) %copy-start.1) | copy-done | bytes 1048600
  4.0 0.0 copy-start.2
  4.0 1.2 %copy-done.2 = bf16[2048,256]{1,0:T(8,128)(2,1)S(1)} copy-done((bf16[2048,256]{1,0:T(8,128)(2,1)S(1)}, bf16[2048,256]{1,0:T(8,128)(2,1)}, u32[]{:S(2)}) %copy-start.2) | copy-done | bytes 1048600
  5.2 0.0 copy-start.4
  5.2 0.8 copy-done.4
  6.0 84.6 %shard_map.122 = (bf16[128,256]{1,0:T(8,128)(2,1)S(1)}, bf16[128,256]{1,0:T(8,128)(2,1)S(1)}) custom-call(bf16[128,256]{1,0:T(8,128)(2,1)S(1)} %copy-done.3, bf16[128,256]{1,0:T(8,128)(2,1)S(1)} %copy-done.4, bf16[2048,256]{1,0:T(8,128)(2,1)S(1)} %copy-done, bf16[2048,256]{1,0:T(8,128)(2,1)S(1)} %copy-done.1, bf16[2048,256]{1,0:T(8,128)(2,1)S(1)} %copy-done.2, ...), custom_call_target="tpu_custom_call" | custom-call | tf_op jit(solution)/shard_map/pallas_call | solution.py:602
  90.6 0.6 copy.15
  91.2 0.6 copy.16
Async XLA Ops:
  0.6 0.8 copy-start.3
  0.6 0.8 copy-start.5
  0.7 0.8 copy-start.6
  0.7 0.8 copy-start.7
  0.7 0.8 copy-start.8
  0.7 0.8 copy-start.9
  1.5 1.2 %copy-start = (bf16[2048,256]{1,0:T(8,128)(2,1)S(1)}, bf16[2048,256]{1,0:T(8,128)(2,1)}, u32[]{:S(2)}) copy-start(bf16[2048,256]{1,0:T(8,128)(2,1)} %w_query.1) | copy-start | bytes 3145732
  2.7 1.2 %copy-start.1 = (bf16[2048,256]{1,0:T(8,128)(2,1)S(1)}, bf16[2048,256]{1,0:T(8,128)(2,1)}, u32[]{:S(2)}) copy-start(bf16[2048,256]{1,0:T(8,128)(2,1)} %w_key.1) | copy-start | bytes 3145732
  4.0 1.2 %copy-start.2 = (bf16[2048,256]{1,0:T(8,128)(2,1)S(1)}, bf16[2048,256]{1,0:T(8,128)(2,1)}, u32[]{:S(2)}) copy-start(bf16[2048,256]{1,0:T(8,128)(2,1)} %w_value.1) | copy-start | bytes 3145732
  5.2 0.8 copy-start.4

commit v2 on v1

--- a/solution.py
+++ b/solution.py
@@ -80,8 +80,7 @@
     clip_lengths,
     delay_offsets,
     block_order,
-    head_out,
-    input_grad,
+    both_out,
     wq,
     wk,
     wv,
@@ -89,8 +88,7 @@
     r1,
     s2,
     r2,
-    arranged,
-    tail,
+    tails,
     feat,
     acc,
     ab,
@@ -163,13 +161,10 @@
             ((w_query, wq), (w_key, wk), (w_value, wv), (out_grad, cot))
         )
     ]
-    for copy in fetches:
-        copy.start()
-
     partners = [at(lax.rem(z + k, Z), g) for k in range(1, Z)]
     partners += [at(z, lax.rem(g + k, G)) for k in range(1, G)]
     partners += [(lax.rem(seq + 1, S), y), (lax.rem(seq + S - 1, S), y)]
-    partners += [(seq, lax.rem(y + 1, H)), (seq, lax.rem(y + H - 1, H))]
+    partners += [(seq, lax.rem(y + k, H)) for k in range(1, H)]
     barrier = pltpu.get_barrier_semaphore()
     for partner in partners:
         pl.semaphore_signal(barrier, inc=1, device_id=partner, device_id_type=pl.DeviceIdType.MESH)
@@ -181,7 +176,12 @@
         to = lax.rem(z + k, Z)
         src = loaded.at[pl.ds(pl.multiple_of(to * rows1, rows1), rows1)]
         copies.append(go(remote(src, r1.at[z], at(to, g))))
-    r1[z] = loaded[pl.ds(pl.multiple_of(z * rows1, rows1), rows1), :]
+    own_rows = loaded.at[pl.ds(pl.multiple_of(z * rows1, rows1), rows1)]
+    keep = pltpu.make_async_copy(own_rows, r1.at[z], local_sem.at[4])
+    keep.start()
+
+    for copy in fetches:
+        copy.start()
 
     first = seq * F
     pos_col = first + iota((F, 1), 0)
@@ -208,6 +208,7 @@
 
     for copy in copies:
         copy.wait_recv()
+    keep.wait()
     s2[...] = dot(regroup, r1[...].reshape(F, W)).astype(BF16).reshape(G, zbr, W)
     copies = []
     for k in range(1, G):
@@ -216,62 +217,65 @@
     r2[g] = s2[g]
     for copy in copies:
         copy.wait_recv()
-    arranged[...] = dot(place, r2[...].reshape(F, W)).astype(BF16)
-
-    halo = go(remote(arranged.at[pl.ds(F - 16, 16)], tail, (lax.rem(seq + 1, S), y)))
+    feat[y] = dot(place, r2[...].reshape(F, W)).astype(BF16)
+
     half = F // 2
-    halves = (half, 0)
-
-    def delayed_rows(start, source_first, source_count):
-        frames = first + start + iota((half, 1), 0)
-        wanted = jnp.where(frames - delay >= begin_col[start : start + half, :], frames - delay, -100)
-        return one_hot(wanted == first + source_first + iota((half, source_count), 1))
-
-    up, down = (seq, lax.rem(y + 1, H)), (seq, lax.rem(y + H - 1, H))
-    hops = (H // 2, H - 1 - H // 2)
-    sign = (-1, 1)
-    gathers = {}
-    for d in range(2):
-        for s in range(hops[d]):
-            for b in range(2):
-                owner = lax.rem(y + sign[d] * s + H, H)
-                part = feat.at[owner, pl.ds(halves[b], half)]
-                gathers[d, s, b] = remote(part, part, (up, down)[d])
-
-    feat[y, half:F, :] = dot(delayed_rows(half, 0, F), arranged[...]).astype(BF16)
-    for d in range(2):
-        if hops[d]:
-            go(gathers[d, 0, 0])
+
+    def ring(k):
+        return lax.rem(y + k + H, H)
+
+    def along(k):
+        return (seq, ring(k))
+
+    halo = go(remote(feat.at[y, pl.ds(F - 16, 16)], tails.at[y], (lax.rem(seq + 1, S), y)))
+    direct = {}
+    for ks in ((2, -2), (1, -1)):
+        for b in range(2):
+            own = feat.at[y, pl.ds(b * half, half)]
+            for k in ks:
+                direct[k, b] = go(remote(own, own, along(k)))
     halo.wait_recv()
-    both = jnp.concatenate([tail[...], arranged[...]], axis=0)
-    feat[y, 0:half, :] = dot(delayed_rows(0, -16, F + 16), both).astype(BF16)
-    for d in range(2):
-        if hops[d]:
-            go(gathers[d, 0, 1])
+    tail_sends = {k: go(remote(tails.at[y], tails.at[y], along(k))) for k in range(1, H)}
 
     def project(owner, begin):
-        block = feat[owner]
+        delay = delay_offsets[lax.div(owner * CB, H)]
+        source = jnp.where(pos_col - delay >= begin_col, iota((F, 1), 0) - delay, -100)
+        shift = one_hot(source == iota((F, F + 16), 1) - 16)
+        block = dot(shift, jnp.concatenate([tails[owner], feat[owner]], axis=0)).astype(BF16)
         here = pl.ds(pl.multiple_of(owner * W, W), W)
         for i, weight in enumerate((wq, wk, wv)):
             value = dot(block, weight[here, :])
             at_cols = slice(i * W, (i + 1) * W)
             acc[:, at_cols] = value if begin else acc[:, at_cols] + value
         value = dot(block, w_beta[:, here], NT)
-        acc[:, 3 * W : 3 * W + 16] = value if begin else acc[:, 3 * W : 3 * W + 16] + value
+        acc[:, 3 * W : 3 * W + 2] = value if begin else acc[:, 3 * W : 3 * W + 2] + value
 
     for copy in fetches:
         copy.wait()
     project(y, True)
-    for s in range(hops[0]):
+    relays = {}
+    for b in range(2):
+        for d in (1, -1):
+            direct[2 * d, b].wait_recv()
+            block = feat.at[ring(-2 * d), pl.ds(b * half, half)]
+            relays[3 * d, b] = go(remote(block, block, along(d)))
+            if b == (0 if d == 1 else 1):
+                relays[4 * d, b] = go(remote(block, block, along(2 * d)))
+    for k in (2, -2, 1, -1):
+        if k in (1, -1):
+            for b in range(2):
+                direct[k, b].wait_recv()
+        tail_sends[k % H].wait_recv()
+        project(ring(-k), False)
+    for k in (3, -3):
         for b in range(2):
-            for d in range(2):
-                if s < hops[d]:
-                    gathers[d, s, b].wait_recv()
-                    if s + 1 < hops[d]:
-                        go(gathers[d, s + 1, b])
-        for d in range(2):
-            if s < hops[d]:
-                project(lax.rem(y + sign[d] * (s + 1) + H, H), False)
+            relays[k, b].wait_recv()
+        tail_sends[k % H].wait_recv()
+        project(ring(-k), False)
+    relays[4, 0].wait_recv()
+    relays[-4, 1].wait_recv()
+    tail_sends[4].wait_recv()
+    project(ring(4), False)
 
     heads = range(2)
     Q, K, V, beta, nq, nk, sig, Gm, T = ({} for _ in range(9))
@@ -395,7 +399,7 @@
         cols = slice(h * N, (h + 1) * N)
         O[h] = Oloc[h] + mm3(R[h], states[h])
         inv = lax.rsqrt(jnp.mean(O[h] * O[h], axis=1, keepdims=True) + EPSILON)
-        head_out[:, cols] = (O[h] * inv * gain).astype(BF16)
+        both_out[0, :, cols] = (O[h] * inv * gain).astype(BF16)
         scaled = cot[:, cols].astype(F32) * gain
         unit = O[h] * inv
         dO[h] = inv * (scaled - unit * jnp.mean(scaled * unit, axis=1, keepdims=True))
@@ -461,7 +465,7 @@
     give_d[...] = jnp.where(core == 0, d_chip, d_early)
     go(remote(give_d, dstates.at[core], sibling)).wait_recv()
 
-    dlog = jnp.zeros((F, 16), F32)
+    dlog = {}
     for h in heads:
         S0, dS = states[h], dstates[h]
         dX = dX0[h] + mm3(Y[h], dS)
@@ -478,49 +482,72 @@
         gcat[:, W + h * N : W + (h + 1) * N] = grad.astype(BF16)
         gcat[:, 2 * W + h * N : 2 * W + (h + 1) * N] = scaled.astype(BF16)
         d_logit = d_beta * beta[h] * (1.0 - sig[h])
-        dlog = dlog + jnp.where(iota((F, 16), 1) == h, d_logit, 0.0)
-    dlog = dlog.astype(BF16)
+        dlog[h] = d_logit.astype(BF16).astype(F32)
 
     def partial(owner):
         here = pl.ds(pl.multiple_of(owner * W, W), W)
-        value = dot(dlog, w_beta[:, here])
+        rows = w_beta[:, here].astype(F32)
+        value = dlog[0] * rows[0:1, :] + dlog[1] * rows[1:2, :]
         for i, weight in enumerate((wq, wk, wv)):
             value = value + dot(gcat[:, i * W : (i + 1) * W], weight[here, :], NT)
         return value
 
-    base = (0, hops[0])
+    hop = (-1, 1, -2, 2, -1, 1, -2, 2)
+    parts = {}
+
+    chunks = ((0, 16), (16, half), (half, F))
+
+    def send_rows(kind, b, value):
+        rows = pl.ds(chunks[b][0], chunks[b][1] - chunks[b][0])
+        src, dst = rs_send.at[kind, rows], rs_recv.at[kind, rows]
+        if kind in (2, 3):
+            src, dst = src.at[:, pl.ds(0, N)], dst.at[:, pl.ds(0, N)]
+            rs_send[kind, rows, :N] = value.astype(BF16)
+        else:
+            rs_send[kind, rows] = value.astype(BF16)
+        reduces[kind, b] = go(remote(src, dst, along(hop[kind])))
+
+    def rows_of(k, b):
+        return parts[k][chunks[b][0] : chunks[b][1], :]
+
+    def received(kind, b):
+        reduces[kind, b].wait_recv()
+        return rs_recv[kind, chunks[b][0] : chunks[b][1], :]
+
     reduces = {}
-    for d in range(2):
-        for s in range(hops[d]):
-            for b in range(2):
-                slot = base[d] + s
-                reduces[d, s, b] = remote(
-                    rs_send.at[slot, b], rs_recv.at[slot, b], (up, down)[d]
-                )
-    for s in range(hops[0]):
-        values = {}
-        for d in range(2):
-            if s < hops[d]:
-                owner = y + hops[0] - s if d == 0 else y - hops[1] + s + H
-                values[d] = partial(lax.rem(owner, H))
-        for b in range(2):
-            for d in range(2):
-                if s < hops[d]:
-                    slot = base[d] + s
-                    value = values[d][b * half : (b + 1) * half, :]
-                    if s:
-                        reduces[d, s - 1, b].wait_recv()
-                        value = value + rs_recv[slot - 1, b].astype(F32)
-                    rs_send[slot, b] = value.astype(BF16)
-                    go(reduces[d, s, b])
-    mine = partial(y)
-    for b in range(2):
-        value = mine[b * half : (b + 1) * half, :]
-        for d in range(2):
-            if hops[d]:
-                reduces[d, hops[d] - 1, b].wait_recv()
-                value = value + rs_recv[base[d] + hops[d] - 1, b].astype(F32)
-        summed[b * half : (b + 1) * half, :] = value.astype(BF16)
+    for k in (-3, 3, 4):
+        parts[k] = partial(ring(k))
+    for b in range(3):
+        send_rows(0, b, rows_of(-3, b))
+        send_rows(1, b, rows_of(3, b))
+        send_rows(2, b, rows_of(4, b)[:, :N])
+        send_rows(3, b, rows_of(4, b)[:, N:])
+    for k in (-1, 1):
+        parts[k] = partial(ring(k))
+    for b in range(3):
+        send_rows(4, b, rows_of(-1, b))
+        send_rows(5, b, rows_of(1, b))
+    for k in (-2, 2, 0):
+        parts[k] = partial(ring(k))
+
+    def hand_on(b):
+        for kind, k in ((6, -2), (7, 2)):
+            value = rows_of(k, b) + received(kind - 6, b).astype(F32)
+            extra = received(kind - 4, b)[:, :N].astype(F32)
+            blank = jnp.zeros_like(extra)
+            extra = jnp.concatenate([extra, blank] if kind == 6 else [blank, extra], axis=1)
+            send_rows(kind, b, value + extra)
+
+    def finish_rows(b):
+        value = rows_of(0, b)
+        for kind in (4, 5, 6, 7):
+            value = value + received(kind, b).astype(F32)
+        summed[chunks[b][0] : chunks[b][1], :] = value.astype(BF16)
+
+    for b in range(3):
+        hand_on(b)
+    for b in range(3):
+        finish_rows(b)
         if b == 0:
             halo = go(remote(summed.at[pl.ds(0, 16)], follow, (lax.rem(seq + S - 1, S), y)))
     ahead = pos_col + delay
@@ -529,7 +556,7 @@
     pull = one_hot(wanted == iota((F, F + 16), 1))
     halo.wait_recv()
     both = jnp.concatenate([summed[...], follow[...]], axis=0)
-    input_grad[...] = dot(pull, both).astype(BF16)
+    both_out[1] = dot(pull, both).astype(BF16)
     for copy in started:
         copy.wait_send()
 
@@ -553,8 +580,6 @@
     G = X * CORES
     BR = F // (Z * G)
     N = 128
-    half = F // 2
-    hops = H - 1
     count = 128
     vmem, smem, anyw = (
         pl.BlockSpec(memory_space=s) for s in (pltpu.VMEM, pltpu.SMEM, pl.ANY)
@@ -568,8 +593,7 @@
         pltpu.VMEM((Z, G * BR, W), BF16),
         pltpu.VMEM((G, Z * BR, W), BF16),
         pltpu.VMEM((G, Z * BR, W), BF16),
-        pltpu.VMEM((F, W), BF16),
-        pltpu.VMEM((16, W), BF16),
+        pltpu.VMEM((H, 16, W), BF16),
         pltpu.VMEM((H, F, W), BF16),
         pltpu.VMEM((F, 3 * W + 128), F32),
         pltpu.VMEM((2, N, 2 * N), F32),
@@ -588,28 +612,24 @@
         pltpu.VMEM((N, N), BF16),
         pltpu.VMEM((2, N, N), F32),
         pltpu.VMEM((F, 3 * W), BF16),
-        pltpu.VMEM((hops, 2, half, W), BF16),
-        pltpu.VMEM((hops, 2, half, W), BF16),
+        pltpu.VMEM((8, F, W), BF16),
+        pltpu.VMEM((8, F, W), BF16),
         pltpu.VMEM((F, W), BF16),
         pltpu.VMEM((16, W), BF16),
         pltpu.VMEM((N, N), F32),
         pltpu.VMEM((N, N), F32),
-        pltpu.SemaphoreType.DMA((4,)),
+        pltpu.SemaphoreType.DMA((5,)),
         pltpu.SemaphoreType.DMA((count,)),
         pltpu.SemaphoreType.DMA((count,)),
     ]
-    wide_beta = jnp.pad(w_beta.T, ((0, 14), (0, 0)))
-    return pl.pallas_call(
+    result = pl.pallas_call(
         functools.partial(kernel, dims),
-        out_shape=(
-            jax.ShapeDtypeStruct((F, W), BF16),
-            jax.ShapeDtypeStruct((F, W), BF16),
-        ),
-        in_specs=[vmem, anyw, anyw, anyw, anyw, vmem, smem, vmem, smem, smem, vmem],
-        out_specs=(vmem, vmem),
+        out_shape=jax.ShapeDtypeStruct((2, F, W), BF16),
+        in_specs=[anyw, anyw, anyw, anyw, anyw, vmem, smem, vmem, smem, smem, vmem],
+        out_specs=vmem,
         scratch_shapes=scratch,
         compiler_params=pltpu.CompilerParams(
-            collective_id=0, has_side_effects=True, vmem_limit_bytes=40 * 2**20
+            collective_id=0, has_side_effects=True, vmem_limit_bytes=60 * 2**20
         ),
     )(
         loaded,
@@ -617,13 +637,14 @@
         w_query,
         w_key,
         w_value,
-        wide_beta,
+        w_beta.T,
         beta_max,
         out_gain.reshape(1, -1),
         clip_lengths,
         delay_offsets,
         block_order,
     )
+    return result[0], result[1]
 
 
 def build(mesh, chips_x, frames):

time: 92.2 us -> 81.2 us (0.88)
  Pallas kernels: 84.6 us -> 78.8 us
  local copies, waits for them, and re-layouts: 6.57 us -> 1.53 us
    unnamed x22 -> x0, local copies, waits for them, and re-layouts: 5.81 us -> none
    pallas_call x1, Pallas kernels: 84.6 us -> 78.8 us  [on_device(): pl.pallas_call(functools.partial(kernel, dims), out_shape=jax.ShapeDtypeS...]
    squeeze x0 -> x1, local copies, waits for them, and re-layouts: none -> 1.53 us  [on_device(): return (result[0], result[1])]
where the time goes in v2:
time: 81.2 us; the launch traced here: 80.9 us
  Pallas kernels  78.8 us (97%)
  local copies, waits for them, and re-layouts  1.53 us (2%)
    pallas_call x1, Pallas kernels, on_device(): pl.pallas_call(functools.partial(kernel, dims), out_shape=jax.ShapeDtypeS...  78.8 us

profile of v2, /device:TPU:1, one launch (start us, length us, event | category | flops | bytes accessed | tf_op | source)
XLA Modules:
  0.0 80.9 jit_solution(5056864481776745412)
XLA Ops:
  0.6 78.8 %shard_map.122 = bf16[2,128,256]{2,1,0:T(8,128)(2,1)} custom-call(bf16[128,256]{1,0:T(8,128)(2,1)} %loaded.1, bf16[128,256]{1,0:T(8,128)(2,1)} %out_grad.1, bf16[2048,256]{1,0:T(8,128)(2,1)} %w_query.1, bf16[2048,256]{1,0:T(8,128)(2,1)} %w_key.1, bf16[2048,256]{1,0:T(8,128)(2,1)} %w_value.1, bf16[2,2048]{1,0:T(2,128)(2,1)} %bitcast.6, f32[2]{0:T(128)} %beta_max.1, ...), custom_call_target="tpu_custom_call" | custom-call | tf_op jit(solution)/shard_map/pallas_call | solution.py:625
  79.4 1.5 %slice_bitcast_fusion = (bf16[128,256]{1,0:T(8,128)(2,1)}, bf16[128,256]{1,0:T(8,128)(2,1)}) fusion(bf16[2,128,256]{2,1,0:T(8,128)(2,1)} %shard_map.122), kind=kLoop, calls=%fused_computation | loop fusion | bytes 262144 | tf_op jit(solution)/shard_map/squeeze | solution.py:647

commit v3 on v2

--- a/solution.py
+++ b/solution.py
@@ -85,34 +85,33 @@
     wk,
     wv,
     cot,
+    s1,
     r1,
     s2,
     r2,
-    tails,
+    last,
+    tail,
     feat,
     acc,
-    ab,
-    sib_ab,
+    raw,
+    pair_raw,
     plane,
     group,
     from_z1,
     from_z2,
     a_next,
-    states,
-    grads,
-    sib_grad,
+    out_pair,
+    out_heads,
     gplane,
     ggroup,
     gz1,
     gz2,
-    dstates,
-    gcat,
+    grad_pair,
+    grad_heads,
     rs_send,
     rs_recv,
     summed,
     follow,
-    give_s,
-    give_d,
     local_sem,
     send_sem,
     recv_sem,
@@ -158,7 +157,7 @@
     fetches = [
         pltpu.make_async_copy(src, dst, local_sem.at[i])
         for i, (src, dst) in enumerate(
-            ((w_query, wq), (w_key, wk), (w_value, wv), (out_grad, cot))
+            ((w_query, wq), (w_key, wk), (w_value, wv))
         )
     ]
     partners = [at(lax.rem(z + k, Z), g) for k in range(1, Z)]
@@ -168,58 +167,68 @@
     barrier = pltpu.get_barrier_semaphore()
     for partner in partners:
         pl.semaphore_signal(barrier, inc=1, device_id=partner, device_id_type=pl.DeviceIdType.MESH)
+
+    rows1, zbr = G * BR, Z * BR
+    row, col = iota((F, F), 0), iota((F, F), 1)
+    to_g, to_z = row // zbr, (row % zbr) // BR
+    regroup = one_hot(col == to_z * rows1 + to_g * BR + row % BR)
+    s1[...] = dot(regroup, loaded[...]).astype(BF16).reshape(G, zbr, W)
     pl.semaphore_wait(barrier, len(partners))
-
-    rows1 = G * BR
+    copies = []
+    for k in range(1, G):
+        to = lax.rem(g + k, G)
+        copies.append(go(remote(s1.at[to], r1.at[g], at(z, to))))
+    r1[g] = s1[g]
+    sibling = at(z, x * C + other)
+
+    def head_columns(h):
+        return out_grad.at[:, pl.ds(pl.multiple_of(h * N, N), N)]
+
+    cot_copy = go(remote(head_columns(other), cot.at[core], sibling))
+    cot_keep = pltpu.make_async_copy(head_columns(core), cot.at[core], local_sem.at[3])
+    cot_keep.start()
+    for copy in fetches:
+        copy.start()
+
+    first = seq * F
+    pos_col = first + iota((F, 1), 0)
+    begin_col = clip_start(clip_lengths, pos_col)
+    delay = delay_offsets[lax.div(y * CB, H)]
+    eye = jnp.where(row == col, 1.0, 0.0)
+    low, low_eq, carried, final, carried_last = ([] for _ in range(5))
+    for i in range(C):
+        start = (seq - core + i) * F
+        at_col = clip_start(clip_lengths, start + iota((F, 1), 0))
+        at_row = clip_start(clip_lengths, start + iota((1, F), 1))
+        same = jnp.where(at_col == at_row, 1.0, 0.0)
+        low.append(jnp.where(row > col, same, 0.0))
+        low_eq.append(jnp.where(row >= col, same, 0.0))
+        carried.append(jnp.where(at_col < start, 1.0, 0.0))
+        final.append(jnp.where(at_col == at_col[F - 1 : F, :], 1.0, 0.0))
+        carried_last.append(carried[i][F - 1 : F, :])
+
+    order = jnp.broadcast_to(block_order[...], (16, S)).astype(F32).astype(BF16)
+    spread = one_hot(iota((S, F), 0) == iota((S, F), 1) // BR)
+    target = dot(order, spread)[0:1, :].astype(jnp.int32) * BR + iota((1, F), 1) % BR
+    place = one_hot(row == target)
+    to_g, to_z = (row % rows1) // BR, row // rows1
+    back_to_z = one_hot(col == to_g * zbr + to_z * BR + row % BR)
+
+    for copy in copies:
+        copy.wait_recv()
+    s2[...] = dot(back_to_z, r1[...].reshape(F, W)).astype(BF16).reshape(Z, rows1, W)
     copies = []
     for k in range(1, Z):
         to = lax.rem(z + k, Z)
-        src = loaded.at[pl.ds(pl.multiple_of(to * rows1, rows1), rows1)]
-        copies.append(go(remote(src, r1.at[z], at(to, g))))
-    own_rows = loaded.at[pl.ds(pl.multiple_of(z * rows1, rows1), rows1)]
-    keep = pltpu.make_async_copy(own_rows, r1.at[z], local_sem.at[4])
-    keep.start()
-
-    for copy in fetches:
-        copy.start()
-
-    first = seq * F
-    pos_col = first + iota((F, 1), 0)
-    begin_col = clip_start(clip_lengths, pos_col)
-    begin_row = clip_start(clip_lengths, first + iota((1, F), 1))
-    delay = delay_offsets[lax.div(y * CB, H)]
-    row, col = iota((F, F), 0), iota((F, F), 1)
-    same = jnp.where(begin_col == begin_row, 1.0, 0.0)
-    low = jnp.where(row > col, same, 0.0)
-    low_eq = jnp.where(row >= col, same, 0.0)
-    eye = jnp.where(row == col, 1.0, 0.0)
-    carried = jnp.where(begin_col < first, 1.0, 0.0)
-    final = jnp.where(begin_col == begin_col[F - 1 : F, :], 1.0, 0.0)
-    carried_last = carried[F - 1 : F, :]
-
-    zbr = Z * BR
-    to_g, to_z, to_r = row // zbr, (row % zbr) // BR, row % BR
-    regroup = one_hot(col == to_z * rows1 + to_g * BR + to_r)
-    order = jnp.broadcast_to(block_order[...], (16, S)).astype(F32).astype(BF16)
-    src_i, out_q = iota((S, F), 0), iota((S, F), 1)
-    spread = one_hot(src_i == ((out_q % zbr) // BR) * G + out_q // zbr)
-    target = dot(order, spread)[0:1, :].astype(jnp.int32) * BR + iota((1, F), 1) % BR
-    place = one_hot(row == target)
-
+        copies.append(go(remote(s2.at[to], r2.at[z], at(to, g))))
+    r2[z] = s2[z]
     for copy in copies:
         copy.wait_recv()
-    keep.wait()
-    s2[...] = dot(regroup, r1[...].reshape(F, W)).astype(BF16).reshape(G, zbr, W)
-    copies = []
-    for k in range(1, G):
-        to = lax.rem(g + k, G)
-        copies.append(go(remote(s2.at[to], r2.at[g], at(z, to))))
-    r2[g] = s2[g]
-    for copy in copies:
-        copy.wait_recv()
-    feat[y] = dot(place, r2[...].reshape(F, W)).astype(BF16)
+    arranged = dot(place, r2[...].reshape(F, W)).astype(BF16)
+    last[...] = arranged[F - 16 :, :]
 
     half = F // 2
+    chunks = ((half, F), (16, half), (0, 16))
 
     def ring(k):
         return lax.rem(y + k + H, H)
@@ -227,21 +236,28 @@
     def along(k):
         return (seq, ring(k))
 
-    halo = go(remote(feat.at[y, pl.ds(F - 16, 16)], tails.at[y], (lax.rem(seq + 1, S), y)))
+    halo = go(remote(last, tail, (lax.rem(seq + 1, S), y)))
+    source = jnp.where(pos_col - delay >= begin_col, iota((F, 1), 0) - delay, -100)
     direct = {}
-    for ks in ((2, -2), (1, -1)):
-        for b in range(2):
-            own = feat.at[y, pl.ds(b * half, half)]
-            for k in ks:
-                direct[k, b] = go(remote(own, own, along(k)))
+
+    def send_own(b):
+        own = feat.at[y, pl.ds(chunks[b][0], chunks[b][1] - chunks[b][0])]
+        for k in (2, -2, 1, -1):
+            direct[k, b] = go(remote(own, own, along(k)))
+
+    shift = one_hot(source == iota((F, F), 1))
+    feat[y, half:, :] = dot(shift[half:, :], arranged).astype(BF16)
+    send_own(0)
+    early = dot(shift[:half, :], arranged)
+    feat[y, 16:half, :] = early[16:, :].astype(BF16)
+    send_own(1)
     halo.wait_recv()
-    tail_sends = {k: go(remote(tails.at[y], tails.at[y], along(k))) for k in range(1, H)}
+    shift = one_hot(source[:16, :] == iota((16, 16), 1) - 16)
+    feat[y, 0:16, :] = (early[:16, :] + dot(shift, tail[...])).astype(BF16)
+    send_own(2)
 
     def project(owner, begin):
-        delay = delay_offsets[lax.div(owner * CB, H)]
-        source = jnp.where(pos_col - delay >= begin_col, iota((F, 1), 0) - delay, -100)
-        shift = one_hot(source == iota((F, F + 16), 1) - 16)
-        block = dot(shift, jnp.concatenate([tails[owner], feat[owner]], axis=0)).astype(BF16)
+        block = feat[owner]
         here = pl.ds(pl.multiple_of(owner * W, W), W)
         for i, weight in enumerate((wq, wk, wv)):
             value = dot(block, weight[here, :])
@@ -254,43 +270,47 @@
         copy.wait()
     project(y, True)
     relays = {}
-    for b in range(2):
+    for b in range(3):
         for d in (1, -1):
             direct[2 * d, b].wait_recv()
-            block = feat.at[ring(-2 * d), pl.ds(b * half, half)]
+            block = feat.at[ring(-2 * d), pl.ds(chunks[b][0], chunks[b][1] - chunks[b][0])]
             relays[3 * d, b] = go(remote(block, block, along(d)))
-            if b == (0 if d == 1 else 1):
+            if (b == 0) == (d == 1):
                 relays[4 * d, b] = go(remote(block, block, along(2 * d)))
     for k in (2, -2, 1, -1):
         if k in (1, -1):
-            for b in range(2):
+            for b in range(3):
                 direct[k, b].wait_recv()
-        tail_sends[k % H].wait_recv()
         project(ring(-k), False)
     for k in (3, -3):
-        for b in range(2):
+        for b in range(3):
             relays[k, b].wait_recv()
-        tail_sends[k % H].wait_recv()
         project(ring(-k), False)
-    relays[4, 0].wait_recv()
-    relays[-4, 1].wait_recv()
-    tail_sends[4].wait_recv()
+    for k, b in ((4, 0), (-4, 1), (-4, 2)):
+        relays[k, b].wait_recv()
     project(ring(4), False)
 
-    heads = range(2)
+    for h in range(C):
+        for i in range(3):
+            raw[h, :, i * N : (i + 1) * N] = acc[:, i * W + h * N : i * W + (h + 1) * N]
+        raw[h, :, 3 * N :] = jnp.broadcast_to(acc[:, 3 * W + h : 3 * W + h + 1], (F, N))
+    copy = go(remote(raw.at[other], pair_raw.at[core], sibling))
+    pair_raw[core] = raw[core]
+    copy.wait_recv()
+
+    both_cores = range(C)
     Q, K, V, beta, nq, nk, sig, Gm, T = ({} for _ in range(9))
-    for h in heads:
-        cols = slice(h * N, (h + 1) * N)
-        q_raw, k_raw = acc[:, cols], acc[:, W + h * N : W + (h + 1) * N]
-        V[h] = acc[:, 2 * W + h * N : 2 * W + (h + 1) * N]
+    for h in both_cores:
+        q_raw, k_raw = pair_raw[h, :, :N], pair_raw[h, :, N : 2 * N]
+        V[h] = pair_raw[h, :, 2 * N : 3 * N]
         nq[h] = lax.rsqrt(jnp.sum(q_raw * q_raw, axis=1, keepdims=True) + EPSILON)
         nk[h] = lax.rsqrt(jnp.sum(k_raw * k_raw, axis=1, keepdims=True) + EPSILON)
         Q[h], K[h] = q_raw * nq[h], k_raw * nk[h]
-        sig[h] = 1.0 / (1.0 + jnp.exp(-acc[:, 3 * W + h : 3 * W + h + 1]))
-        beta[h] = beta_max[h] * sig[h]
+        sig[h] = 1.0 / (1.0 + jnp.exp(-pair_raw[h, :, 3 * N : 3 * N + 1]))
+        beta[h] = beta_max[core] * sig[h]
     L = {}
-    for h in heads:
-        Gm[h] = mm3(K[h], K[h], NT) * low
+    for h in both_cores:
+        Gm[h] = mm3(K[h], K[h], NT) * low[h]
         L[h] = beta[h] * Gm[h]
     size = 1
     while size < F:
@@ -299,43 +319,35 @@
             & ((row // size) % 2 == 1)
             & ((col // size) % 2 == 0)
         )
-        inner = {h: jnp.where(pair, L[h], 0.0) for h in heads}
+        inner = {h: jnp.where(pair, L[h], 0.0) for h in both_cores}
         if size == 1:
-            T = {h: eye - inner[h] for h in heads}
+            T = {h: eye - inner[h] for h in both_cores}
         else:
-            half_way = {h: mm3(T[h], inner[h]) for h in heads}
-            T = {h: T[h] - mm3(half_way[h], T[h]) for h in heads}
+            half_way = {h: mm3(T[h], inner[h]) for h in both_cores}
+            T = {h: T[h] - mm3(half_way[h], T[h]) for h in both_cores}
         size *= 2
-    Wk, Wv = {}, {}
-    for h in heads:
+    Wk, Wv, A, B = {}, {}, {}, {}
+    for h in both_cores:
         both = mm3(T[h], beta[h] * jnp.concatenate([K[h], V[h]], axis=1))
         Wk[h], Wv[h] = both[:, :N], both[:, N:]
-    for h in heads:
-        both = mm3(K[h], jnp.concatenate([Wk[h], final * Wv[h]], axis=1), TN)
-        ab[h, :, :N] = carried_last * (eye - both[:, :N])
-        ab[h, :, N:] = both[:, N:]
-
-    sibling = at(z, x * C + other)
-    copy = go(remote(ab.at[other], sib_ab, sibling))
-    P_, Oloc, R = {}, {}, {}
-    for h in heads:
-        P_[h] = mm3(Q[h], K[h], NT) * low_eq
-        both = mm3(P_[h], jnp.concatenate([carried * Wk[h], Wv[h]], axis=1))
-        R[h] = carried * Q[h] - both[:, :N]
-        Oloc[h] = both[:, N:]
-    copy.wait_recv()
-    own, sib = ab[core], sib_ab[...]
-    early = jnp.where(core == 0, own, sib)
-    late = jnp.where(core == 0, sib, own)
-    a_early, b_early = early[:, :N], early[:, N:]
-    a_late, b_late = late[:, :N], late[:, N:]
+    for h in both_cores:
+        both = mm3(K[h], jnp.concatenate([Wk[h], final[h] * Wv[h]], axis=1), TN)
+        A[h] = carried_last[h] * (eye - both[:, :N])
+        B[h] = both[:, N:]
+
     zero = jnp.zeros((N, N), F32)
-    pad_b = jnp.concatenate([zero, b_late], axis=1)
-    plane[x] = (mm3(a_late, early) + pad_b).astype(BF16)
+    pad_b = jnp.concatenate([zero, B[1]], axis=1)
+    plane[x] = (mm3(A[1], jnp.concatenate([A[0], B[0]], axis=1)) + pad_b).astype(BF16)
     copies = []
     for k in range(1, X):
         to = lax.rem(x + k, X)
         copies.append(go(remote(plane.at[x], plane.at[x], at(z, to * C + core))))
+    P_, Oloc, R = {}, {}, {}
+    for h in both_cores:
+        P_[h] = mm3(Q[h], K[h], NT) * low_eq[h]
+        both = mm3(P_[h], jnp.concatenate([carried[h] * Wk[h], Wv[h]], axis=1))
+        R[h] = carried[h] * Q[h] - both[:, :N]
+        Oloc[h] = both[:, N:]
     for copy in copies:
         copy.wait_recv()
 
@@ -388,41 +400,33 @@
         copy.wait_recv()
     s_group = from_z1[:, N:].astype(F32) + dot(from_z1[:, :N], from_z2[...])
     s_chip = before_me[:, N:] + mm3(before_me[:, :N], s_group)
-    s_late = b_early + mm3(a_early, s_chip)
-    states[core] = jnp.where(core == 0, s_chip, s_late)
-    give_s[...] = jnp.where(core == 0, s_late, s_chip)
-    go(remote(give_s, states.at[core], sibling)).wait_recv()
+    state = (s_chip, B[0] + mm3(A[0], s_chip))
 
     gain = out_gain[...]
-    O, dO = {}, {}
-    for h in heads:
-        cols = slice(h * N, (h + 1) * N)
-        O[h] = Oloc[h] + mm3(R[h], states[h])
+    O, dO, ask = {}, {}, {}
+    cot_copy.wait_recv()
+    cot_keep.wait()
+    for h in both_cores:
+        O[h] = Oloc[h] + mm3(R[h], state[h])
         inv = lax.rsqrt(jnp.mean(O[h] * O[h], axis=1, keepdims=True) + EPSILON)
-        both_out[0, :, cols] = (O[h] * inv * gain).astype(BF16)
-        scaled = cot[:, cols].astype(F32) * gain
+        out_pair[h] = (O[h] * inv * gain).astype(BF16)
+        scaled = cot[h].astype(F32) * gain
         unit = O[h] * inv
         dO[h] = inv * (scaled - unit * jnp.mean(scaled * unit, axis=1, keepdims=True))
-        grads[h] = mm3(R[h], dO[h], TN)
-    copy = go(remote(grads.at[other], sib_grad, sibling))
-    U, dU0, Y, dX0, dP, dQ, dK0, Zv = ({} for _ in range(8))
-    for h in heads:
-        S0 = states[h]
-        KS = carried * mm3(K[h], S0)
-        Zv[h] = V[h] - KS
-        U[h] = Wv[h] - carried * mm3(Wk[h], S0)
-    copy.wait_recv()
-    own, sib = grads[core], sib_grad[...]
-    g_early = jnp.where(core == 0, own, sib)
-    g_late = jnp.where(core == 0, sib, own)
-    gplane[x] = (g_early + mm3(a_early, g_late, TN)).astype(BF16)
+        ask[h] = mm3(R[h], dO[h], TN)
+    gplane[x] = (ask[0] + mm3(A[0], ask[1], TN)).astype(BF16)
     copies = []
     for k in range(1, X):
         to = lax.rem(x + k, X)
         copies.append(go(remote(gplane.at[x], gplane.at[x], at(z, to * C + core))))
-    for h in heads:
+    out_copy = go(remote(out_pair.at[other], out_heads.at[core], sibling))
+    out_heads[core] = out_pair[core]
+    U, dU0, Y, dX0, dP, dQ, dK0, Zv = ({} for _ in range(8))
+    for h in both_cores:
+        Zv[h] = V[h] - carried[h] * mm3(K[h], state[h])
+        U[h] = Wv[h] - carried[h] * mm3(Wk[h], state[h])
         dU0[h] = mm3(P_[h], dO[h], TN)
-        both = mm3(T[h], jnp.concatenate([dU0[h], final * K[h]], axis=1), TN)
+        both = mm3(T[h], jnp.concatenate([dU0[h], final[h] * K[h]], axis=1), TN)
         dX0[h], Y[h] = both[:, :N], both[:, N:]
     for copy in copies:
         copy.wait_recv()
@@ -448,48 +452,49 @@
         go(remote(ggroup, gz2, at(y2, g))),
     ]
     behind_me = pick(behind, x)
-    for h in heads:
-        S0 = states[h]
-        dP[h] = mm3(dO[h], U[h], NT) * low_eq
-        dQ[h] = carried * mm3(dO[h], S0, NT) + mm3(dP[h], K[h])
+    for h in both_cores:
+        dP[h] = mm3(dO[h], U[h], NT) * low_eq[h]
+        dQ[h] = carried[h] * mm3(dO[h], state[h], NT) + mm3(dP[h], K[h])
         dK0[h] = mm3(dP[h], Q[h], TN)
         grad = nq[h] * (dQ[h] - Q[h] * jnp.sum(Q[h] * dQ[h], axis=1, keepdims=True))
-        gcat[:, h * N : (h + 1) * N] = grad.astype(BF16)
+        grad_pair[h, :, :N] = grad.astype(BF16)
     next_copy.wait_recv()
     for copy in copies:
         copy.wait_recv()
     d_group = gz1[...].astype(F32) + dot(a_next[...], gz2[...], TN)
     d_chip = behind_me + mm3(after_me, d_group, TN)
-    d_early = g_late + mm3(a_late, d_chip, TN)
-    dstates[core] = jnp.where(core == 0, d_early, d_chip)
-    give_d[...] = jnp.where(core == 0, d_chip, d_early)
-    go(remote(give_d, dstates.at[core], sibling)).wait_recv()
-
-    dlog = {}
-    for h in heads:
-        S0, dS = states[h], dstates[h]
-        dX = dX0[h] + mm3(Y[h], dS)
-        scaled = beta[h] * dX
-        both = mm3(dX, jnp.concatenate([U[h], S0], axis=0), NT)
-        dL = -both[:, :F] * low
+    d_state = (ask[1] + mm3(A[1], d_chip, TN), d_chip)
+
+    for h in both_cores:
+        dX = dX0[h] + mm3(Y[h], d_state[h])
+        both = mm3(dX, jnp.concatenate([U[h], state[h]], axis=0), NT)
+        dL = -both[:, :F] * low[h]
         dG = beta[h] * dL
-        dK = dK0[h] + mm3(final * U[h], dS, NT)
-        dK = dK - carried * beta[h] * both[:, F:]
+        dK = dK0[h] + mm3(final[h] * U[h], d_state[h], NT)
+        dK = dK - carried[h] * beta[h] * both[:, F:]
         dK = dK + mm3(dG, K[h]) + mm3(dG, K[h], TN)
         d_beta = jnp.sum(dX * Zv[h], axis=1, keepdims=True)
         d_beta = d_beta + jnp.sum(dL * Gm[h], axis=1, keepdims=True)
         grad = nk[h] * (dK - K[h] * jnp.sum(K[h] * dK, axis=1, keepdims=True))
-        gcat[:, W + h * N : W + (h + 1) * N] = grad.astype(BF16)
-        gcat[:, 2 * W + h * N : 2 * W + (h + 1) * N] = scaled.astype(BF16)
         d_logit = d_beta * beta[h] * (1.0 - sig[h])
-        dlog[h] = d_logit.astype(BF16).astype(F32)
+        grad_pair[h, :, N : 2 * N] = grad.astype(BF16)
+        grad_pair[h, :, 2 * N : 3 * N] = (beta[h] * dX).astype(BF16)
+        grad_pair[h, :, 3 * N :] = jnp.broadcast_to(d_logit, (F, N)).astype(BF16)
+    copy = go(remote(grad_pair.at[other], grad_heads.at[core], sibling))
+    grad_heads[core] = grad_pair[core]
+    copy.wait_recv()
+    wide = [
+        jnp.concatenate([grad_heads[h, :, i * N : (i + 1) * N] for h in range(C)], axis=1)
+        for i in range(3)
+    ]
+    dlog = [grad_heads[h, :, 3 * N : 3 * N + 1].astype(F32) for h in range(C)]
 
     def partial(owner):
         here = pl.ds(pl.multiple_of(owner * W, W), W)
         rows = w_beta[:, here].astype(F32)
         value = dlog[0] * rows[0:1, :] + dlog[1] * rows[1:2, :]
         for i, weight in enumerate((wq, wk, wv)):
-            value = value + dot(gcat[:, i * W : (i + 1) * W], weight[here, :], NT)
+            value = value + dot(wide[i], weight[here, :], NT)
         return value
 
     hop = (-1, 1, -2, 2, -1, 1, -2, 2)
@@ -557,6 +562,9 @@
     halo.wait_recv()
     both = jnp.concatenate([summed[...], follow[...]], axis=0)
     both_out[1] = dot(pull, both).astype(BF16)
+    out_copy.wait_recv()
+    for h in range(C):
+        both_out[0, :, h * N : (h + 1) * N] = out_heads[h]
     for copy in started:
         copy.wait_send()
 
@@ -589,43 +597,42 @@
         pltpu.VMEM((D, W), BF16),
         pltpu.VMEM((D, W), BF16),
         pltpu.VMEM((D, W), BF16),
-        pltpu.VMEM((F, W), BF16),
-        pltpu.VMEM((Z, G * BR, W), BF16),
+        pltpu.VMEM((2, F, N), BF16),
         pltpu.VMEM((G, Z * BR, W), BF16),
         pltpu.VMEM((G, Z * BR, W), BF16),
-        pltpu.VMEM((H, 16, W), BF16),
+        pltpu.VMEM((Z, G * BR, W), BF16),
+        pltpu.VMEM((Z, G * BR, W), BF16),
+        pltpu.VMEM((16, W), BF16),
+        pltpu.VMEM((16, W), BF16),
         pltpu.VMEM((H, F, W), BF16),
         pltpu.VMEM((F, 3 * W + 128), F32),
-        pltpu.VMEM((2, N, 2 * N), F32),
-        pltpu.VMEM((N, 2 * N), F32),
+        pltpu.VMEM((2, F, 4 * N), F32),
+        pltpu.VMEM((2, F, 4 * N), F32),
         pltpu.VMEM((X, N, 2 * N), BF16),
         pltpu.VMEM((N, 2 * N), BF16),
         pltpu.VMEM((N, 2 * N), BF16),
         pltpu.VMEM((N, N), BF16),
         pltpu.VMEM((N, N), BF16),
-        pltpu.VMEM((2, N, N), F32),
-        pltpu.VMEM((2, N, N), F32),
-        pltpu.VMEM((N, N), F32),
+        pltpu.VMEM((2, F, N), BF16),
+        pltpu.VMEM((2, F, N), BF16),
         pltpu.VMEM((X, N, N), BF16),
         pltpu.VMEM((N, N), BF16),
         pltpu.VMEM((N, N), BF16),
         pltpu.VMEM((N, N), BF16),
-        pltpu.VMEM((2, N, N), F32),
-        pltpu.VMEM((F, 3 * W), BF16),
+        pltpu.VMEM((2, F, 4 * N), BF16),
+        pltpu.VMEM((2, F, 4 * N), BF16),
         pltpu.VMEM((8, F, W), BF16),
         pltpu.VMEM((8, F, W), BF16),
         pltpu.VMEM((F, W), BF16),
         pltpu.VMEM((16, W), BF16),
-        pltpu.VMEM((N, N), F32),
-        pltpu.VMEM((N, N), F32),
-        pltpu.SemaphoreType.DMA((5,)),
+        pltpu.SemaphoreType.DMA((4,)),
         pltpu.SemaphoreType.DMA((count,)),
         pltpu.SemaphoreType.DMA((count,)),
     ]
     result = pl.pallas_call(
         functools.partial(kernel, dims),
         out_shape=jax.ShapeDtypeStruct((2, F, W), BF16),
-        in_specs=[anyw, anyw, anyw, anyw, anyw, vmem, smem, vmem, smem, smem, vmem],
+        in_specs=[vmem, anyw, anyw, anyw, anyw, vmem, smem, vmem, smem, smem, vmem],
         out_specs=vmem,
         scratch_shapes=scratch,
         compiler_params=pltpu.CompilerParams(

time: 81.2 us -> 78.3 us (0.964)
  Pallas kernels: 78.8 us -> 76 us
    pallas_call x1, Pallas kernels: 78.8 us -> 76 us  [on_device(): pl.pallas_call(functools.partial(kernel, dims), out_shape=jax.ShapeDtypeS...]
where the time goes in v3:
time: 78.3 us; the launch traced here: 78.1 us
  Pallas kernels  76 us (97%)
  local copies, waits for them, and re-layouts  1.53 us (2%)
    pallas_call x1, Pallas kernels, on_device(): pl.pallas_call(functools.partial(kernel, dims), out_shape=jax.ShapeDtypeS...  76 us

profile of v3, /device:TPU:1, one launch (start us, length us, event | category | flops | bytes accessed | tf_op | source)
XLA Modules:
  0.0 78.1 jit_solution(2251192397386855262)
XLA Ops:
  0.6 76.0 %shard_map.122 = bf16[2,128,256]{2,1,0:T(8,128)(2,1)} custom-call(bf16[128,256]{1,0:T(8,128)(2,1)} %loaded.1, bf16[128,256]{1,0:T(8,128)(2,1)} %out_grad.1, bf16[2048,256]{1,0:T(8,128)(2,1)} %w_query.1, bf16[2048,256]{1,0:T(8,128)(2,1)} %w_key.1, bf16[2048,256]{1,0:T(8,128)(2,1)} %w_value.1, bf16[2,2048]{1,0:T(2,128)(2,1)} %bitcast.6, f32[2]{0:T(128)} %beta_max.1, ...), custom_call_target="tpu_custom_call" | custom-call | tf_op jit(solution)/shard_map/pallas_call | solution.py:632
  76.6 1.5 %slice_bitcast_fusion = (bf16[128,256]{1,0:T(8,128)(2,1)}, bf16[128,256]{1,0:T(8,128)(2,1)}) fusion(bf16[2,128,256]{2,1,0:T(8,128)(2,1)} %shard_map.122), kind=kLoop, calls=%fused_computation | loop fusion | bytes 262144 | tf_op jit(solution)/shard_map/squeeze | solution.py:654

commit v4 on v3

--- a/solution.py
+++ b/solution.py
@@ -69,18 +69,25 @@
 
 def kernel(
     dims,
-    loaded,
+    loaded_hbm,
     out_grad,
     w_query,
     w_key,
     w_value,
+    w_beta_hbm,
+    beta_max_hbm,
+    out_gain_hbm,
+    clip_lengths_hbm,
+    delay_offsets_hbm,
+    block_order_hbm,
+    both_out,
+    loaded,
     w_beta,
     beta_max,
     out_gain,
     clip_lengths,
     delay_offsets,
     block_order,
-    both_out,
     wq,
     wk,
     wv,
@@ -112,6 +119,7 @@
     rs_recv,
     summed,
     follow,
+    summed_out,
     local_sem,
     send_sem,
     recv_sem,
@@ -167,11 +175,28 @@
     barrier = pltpu.get_barrier_semaphore()
     for partner in partners:
         pl.semaphore_signal(barrier, inc=1, device_id=partner, device_id_type=pl.DeviceIdType.MESH)
+    small = [
+        pltpu.make_async_copy(src, dst, local_sem.at[4 + i])
+        for i, (src, dst) in enumerate(
+            (
+                (loaded_hbm, loaded),
+                (clip_lengths_hbm, clip_lengths),
+                (delay_offsets_hbm, delay_offsets),
+                (block_order_hbm, block_order),
+                (beta_max_hbm, beta_max),
+                (out_gain_hbm, out_gain),
+                (w_beta_hbm, w_beta),
+            )
+        )
+    ]
+    for copy in small:
+        copy.start()
 
     rows1, zbr = G * BR, Z * BR
     row, col = iota((F, F), 0), iota((F, F), 1)
     to_g, to_z = row // zbr, (row % zbr) // BR
     regroup = one_hot(col == to_z * rows1 + to_g * BR + row % BR)
+    small[0].wait()
     s1[...] = dot(regroup, loaded[...]).astype(BF16).reshape(G, zbr, W)
     pl.semaphore_wait(barrier, len(partners))
     copies = []
@@ -190,6 +215,8 @@
     for copy in fetches:
         copy.start()
 
+    for copy in small[1:]:
+        copy.wait()
     first = seq * F
     pos_col = first + iota((F, 1), 0)
     begin_col = clip_start(clip_lengths, pos_col)
@@ -458,6 +485,15 @@
         dK0[h] = mm3(dP[h], Q[h], TN)
         grad = nq[h] * (dQ[h] - Q[h] * jnp.sum(Q[h] * dQ[h], axis=1, keepdims=True))
         grad_pair[h, :, :N] = grad.astype(BF16)
+    out_copy.wait_recv()
+    head_outs = [
+        pltpu.make_async_copy(
+            out_heads.at[h], both_out.at[0, :, pl.ds(h * N, N)], local_sem.at[12 + h]
+        )
+        for h in range(C)
+    ]
+    for copy in head_outs:
+        copy.start()
     next_copy.wait_recv()
     for copy in copies:
         copy.wait_recv()
@@ -561,12 +597,14 @@
     pull = one_hot(wanted == iota((F, F + 16), 1))
     halo.wait_recv()
     both = jnp.concatenate([summed[...], follow[...]], axis=0)
-    both_out[1] = dot(pull, both).astype(BF16)
-    out_copy.wait_recv()
-    for h in range(C):
-        both_out[0, :, h * N : (h + 1) * N] = out_heads[h]
+    summed_out[...] = dot(pull, both).astype(BF16)
+    last_out = pltpu.make_async_copy(summed_out, both_out.at[1], local_sem.at[11])
+    last_out.start()
     for copy in started:
         copy.wait_send()
+    for copy in head_outs:
+        copy.wait()
+    last_out.wait()
 
 
 def on_device(
@@ -589,11 +627,16 @@
     BR = F // (Z * G)
     N = 128
     count = 128
-    vmem, smem, anyw = (
-        pl.BlockSpec(memory_space=s) for s in (pltpu.VMEM, pltpu.SMEM, pl.ANY)
-    )
+    anyw = pl.BlockSpec(memory_space=pl.ANY)
     D = w_query.shape[0]
     scratch = [
+        pltpu.VMEM((F, W), BF16),
+        pltpu.VMEM((2, D), BF16),
+        pltpu.SMEM(beta_max.shape, F32),
+        pltpu.VMEM((1, N), F32),
+        pltpu.SMEM(clip_lengths.shape, jnp.int32),
+        pltpu.SMEM(delay_offsets.shape, jnp.int32),
+        pltpu.VMEM(block_order.shape, jnp.int32),
         pltpu.VMEM((D, W), BF16),
         pltpu.VMEM((D, W), BF16),
         pltpu.VMEM((D, W), BF16),
@@ -625,15 +668,16 @@
         pltpu.VMEM((8, F, W), BF16),
         pltpu.VMEM((F, W), BF16),
         pltpu.VMEM((16, W), BF16),
-        pltpu.SemaphoreType.DMA((4,)),
+        pltpu.VMEM((F, W), BF16),
+        pltpu.SemaphoreType.DMA((16,)),
         pltpu.SemaphoreType.DMA((count,)),
         pltpu.SemaphoreType.DMA((count,)),
     ]
     result = pl.pallas_call(
         functools.partial(kernel, dims),
         out_shape=jax.ShapeDtypeStruct((2, F, W), BF16),
-        in_specs=[vmem, anyw, anyw, anyw, anyw, vmem, smem, vmem, smem, smem, vmem],
-        out_specs=vmem,
+        in_specs=[anyw] * 11,
+        out_specs=anyw,
         scratch_shapes=scratch,
         compiler_params=pltpu.CompilerParams(
             collective_id=0, has_side_effects=True, vmem_limit_bytes=60 * 2**20

time: 78.3 us -> 77 us (0.983)
  Pallas kernels: 76 us -> 74.6 us
    pallas_call x1, Pallas kernels: 76 us -> 74.6 us  [on_device(): pl.pallas_call(functools.partial(kernel, dims), out_shape=jax.ShapeDtypeS...]
where the time goes in v4:
time: 77 us; the launch traced here: 76.8 us
  Pallas kernels  74.6 us (97%)
  local copies, waits for them, and re-layouts  1.53 us (2%)
    pallas_call x1, Pallas kernels, on_device(): pl.pallas_call(functools.partial(kernel, dims), out_shape=jax.ShapeDtypeS...  74.6 us

profile of v4, /device:TPU:1, one launch (start us, length us, event | category | flops | bytes accessed | tf_op | source)
XLA Modules:
  0.0 76.8 jit_solution(15921652125738899291)
XLA Ops:
  0.6 74.6 %shard_map.122 = bf16[2,128,256]{2,1,0:T(8,128)(2,1)} custom-call(bf16[128,256]{1,0:T(8,128)(2,1)} %loaded_hbm.1, bf16[128,256]{1,0:T(8,128)(2,1)} %out_grad.1, bf16[2048,256]{1,0:T(8,128)(2,1)} %w_query.1, bf16[2048,256]{1,0:T(8,128)(2,1)} %w_key.1, bf16[2048,256]{1,0:T(8,128)(2,1)} %w_value.1, bf16[2,2048]{1,0:T(2,128)(2,1)} %bitcast.6, f32[2]{0:T(128)} %beta_max_hbm.1, ...), custom_call_target="tpu_custom_call" | custom-call | tf_op jit(solution)/shard_map/pallas_call | solution.py:676
  75.3 1.5 %slice_bitcast_fusion = (bf16[128,256]{1,0:T(8,128)(2,1)}, bf16[128,256]{1,0:T(8,128)(2,1)}) fusion(bf16[2,128,256]{2,1,0:T(8,128)(2,1)} %shard_map.122), kind=kLoop, calls=%fused_computation | loop fusion | bytes 262144 | tf_op jit(solution)/shard_map/squeeze | solution.py:698

commit v5 on v4

--- a/solution.py
+++ b/solution.py
@@ -556,18 +556,14 @@
         return rs_recv[kind, chunks[b][0] : chunks[b][1], :]
 
     reduces = {}
-    for k in (-3, 3, 4):
+    for k, kinds in ((-3, (0,)), (3, (1,)), (4, (2, 3)), (-1, (4,)), (1, (5,))):
         parts[k] = partial(ring(k))
-    for b in range(3):
-        send_rows(0, b, rows_of(-3, b))
-        send_rows(1, b, rows_of(3, b))
-        send_rows(2, b, rows_of(4, b)[:, :N])
-        send_rows(3, b, rows_of(4, b)[:, N:])
-    for k in (-1, 1):
-        parts[k] = partial(ring(k))
-    for b in range(3):
-        send_rows(4, b, rows_of(-1, b))
-        send_rows(5, b, rows_of(1, b))
+        for b in range(3):
+            for kind in kinds:
+                value = rows_of(k, b)
+                if k == 4:
+                    value = value[:, :N] if kind == 2 else value[:, N:]
+                send_rows(kind, b, value)
     for k in (-2, 2, 0):
         parts[k] = partial(ring(k))
 

time: 77 us -> 77.2 us (level)
  no operation moved by 1% of the time
where the time goes in v5:
time: 77.2 us; the launch traced here: 76.8 us
  Pallas kernels  74.6 us (97%)
  local copies, waits for them, and re-layouts  1.53 us (2%)
    pallas_call x1, Pallas kernels, on_device(): pl.pallas_call(functools.partial(kernel, dims), out_shape=jax.ShapeDtypeS...  74.6 us

profile of v5, /device:TPU:1, one launch (start us, length us, event | category | flops | bytes accessed | tf_op | source)
XLA Modules:
  0.0 76.8 jit_solution(12990037438297542060)
XLA Ops:
  0.6 74.6 %shard_map.122 = bf16[2,128,256]{2,1,0:T(8,128)(2,1)} custom-call(bf16[128,256]{1,0:T(8,128)(2,1)} %loaded_hbm.1, bf16[128,256]{1,0:T(8,128)(2,1)} %out_grad.1, bf16[2048,256]{1,0:T(8,128)(2,1)} %w_query.1, bf16[2048,256]{1,0:T(8,128)(2,1)} %w_key.1, bf16[2048,256]{1,0:T(8,128)(2,1)} %w_value.1, bf16[2,2048]{1,0:T(2,128)(2,1)} %bitcast.6, f32[2]{0:T(128)} %beta_max_hbm.1, ...), custom_call_target="tpu_custom_call" | custom-call | tf_op jit(solution)/shard_map/pallas_call | solution.py:672
  75.2 1.5 %slice_bitcast_fusion = (bf16[128,256]{1,0:T(8,128)(2,1)}, bf16[128,256]{1,0:T(8,128)(2,1)}) fusion(bf16[2,128,256]{2,1,0:T(8,128)(2,1)} %shard_map.122), kind=kLoop, calls=%fused_computation | loop fusion | bytes 262144 | tf_op jit(solution)/shard_map/squeeze | solution.py:694
